TPU v7x, 128 devices: a whole 4x4x4 slice. The times are simulated.
128 devices in a mesh: lat: 4 (over z_lo, core), lon: 32 (over y, x, z_hi).
Axes of the slice: x: 4, y: 4, z: 4 (z_hi: 2, z_lo: 2; z = z_hi * 2 + z_lo), core: 2. Of those that a mesh axis runs over, the one named last changes fastest.
Arguments:
- fields_in: bfloat16 [8, 32, 1024, 512], P('lat', 'lon'), may hold values from -6 to 6
- lon_operator: bfloat16 [1024, 1024], replicated, may hold values from -0.1875 to 0.1875
- w_in: bfloat16 [512, 256], replicated, may hold values from -0.375 to 0.375
- w_out: bfloat16 [256, 512], replicated, may hold values from -0.25 to 0.25
- inverses: bfloat16 [4, 32, 32, 32, 4096], P('lat', 'lon'), may hold values from -0.5 to 1.4, as said below
- cotangent: bfloat16 [4, 32, 8, 32, 4096], P('lat', 'lon'), may hold values from -6 to 6
Outputs:
- diffused: float32 [4, 32, 8, 32, 4096], P('lat', 'lon')
- grad_fields: float32 [8, 32, 1024, 512], P('lat', 'lon')
- grad_in: float32 [512, 256], replicated
- grad_out: float32 [256, 512], replicated
Inputs may be any that keep to these rules, and one draw needn't show every extreme that they name: `inverses`: the diagonal of each matrix lies between 0.6 and 1.4.
All inputs are finite; a program needn't handle non-finite values.
Results may differ from a plain program's by a relative error of at most 0.0055.
Values may be sent and summed in bfloat16 or wider, within the bound.
No kernel may reach another device: no remote copies, remote signals or barrier semaphores. Data moves between devices by JAX's collectives and lax.ppermute only.
A program may use at most 192 MiB of HBM per device.

v0:
```python
import functools

import jax
import jax.numpy as jnp
from jax import lax
from jax.experimental import pallas as pl
from jax.experimental.pallas import tpu as pltpu
from jax.sharding import PartitionSpec as P

KAPPA = 0.2
AXES = ("lat", "lon")
BF = jnp.bfloat16
F32 = jnp.float32
LANES = 128
QROWS = 8
VMEM_LIMIT = 60 * 1024 * 1024


def params():
    return pltpu.CompilerParams(vmem_limit_bytes=VMEM_LIMIT)


def cost(flops, nbytes, trans=0):
    return pl.CostEstimate(flops=int(flops), bytes_accessed=int(nbytes), transcendentals=int(trans))


def dot(a, b, dims=(1, 0)):
    return lax.dot_general(a, b, (((dims[0],), (dims[1],)), ((), ())), preferred_element_type=F32)


def meridional(wide):
    size = wide.shape[1]
    lane = lax.broadcasted_iota(jnp.int32, wide.shape, 1)
    before = jnp.where(lane == 0, 0.0, pltpu.roll(wide, 1, 1))
    after = jnp.where(lane == size - 1, 0.0, pltpu.roll(wide, size - 1, 1))
    return after + before - 2.0 * wide


def forward_kernel(v_ref, op_ref, out_ref, *, block):
    step = pl.program_id(0)
    rows = pl.ds(pl.multiple_of(step * block, block), block)
    fields = v_ref.shape[0]
    tiles, tile_lon, chunks = out_ref.shape[0], out_ref.shape[1], out_ref.shape[2]
    done = []
    for f in range(fields):
        along = dot(op_ref[...], v_ref[f], (0, 0))
        wide = v_ref[f, rows, :].astype(F32)
        done.append(wide + along + KAPPA * meridional(wide))
    for a in range(tiles):
        parts = [
            d[:, a * LANES : (a + 1) * LANES].reshape(tile_lon, chunks, 1, QROWS, LANES) for d in done
        ]
        joined = jnp.concatenate(parts, axis=2).reshape(tile_lon, chunks, fields * QROWS, LANES)
        out_ref[a] = joined.astype(BF)


def forward(fields_in, operator, lat_tiles, lon_tiles, tile_lon):
    fields, grid_lon, grid_lat = fields_in.shape
    chunks = tile_lon // QROWS
    block = 256
    out_shape = (lat_tiles, lon_tiles, chunks, fields * QROWS, LANES)
    return pl.pallas_call(
        functools.partial(forward_kernel, block=block),
        grid=(grid_lon // block,),
        in_specs=[
            pl.BlockSpec((fields, grid_lon, grid_lat), lambda i: (0, 0, 0)),
            pl.BlockSpec((grid_lon, block), lambda i: (0, i)),
        ],
        out_specs=pl.BlockSpec(
            (lat_tiles, block // tile_lon) + out_shape[2:], lambda i: (0, i, 0, 0, 0)
        ),
        out_shape=jax.ShapeDtypeStruct(out_shape, BF),
        compiler_params=params(),
        cost_estimate=cost(2 * fields * grid_lon * grid_lon * grid_lat, 6 << 20),
        name="forward_dynamics",
    )(fields_in, operator)


def grad_mixed_kernel(inv_ref, cot_ref, out_ref, wide):
    levels = inv_ref.shape[0]
    fields = cot_ref.shape[0] // levels
    wide[...] = cot_ref[...].astype(F32)

    def tile(t, carry):
        lanes = pl.ds(pl.multiple_of(t * LANES, LANES), LANES)
        acc = [None] * fields
        for l in range(levels):
            matrix = inv_ref[l, :, lanes].astype(F32)
            for f in range(fields):
                term = matrix * wide[pl.ds(f * levels + l, 1), lanes]
                acc[f] = term if acc[f] is None else acc[f] + term
        for f in range(fields):
            out_ref[f * levels : (f + 1) * levels, lanes] = acc[f]
        return carry

    lax.fori_loop(0, inv_ref.shape[2] // LANES, tile, 0)


def grad_mixed_of(matrix, incoming):
    levels, _, columns = matrix.shape
    values = incoming.shape[0]
    chunk = 512
    return pl.pallas_call(
        grad_mixed_kernel,
        grid=(columns // chunk,),
        in_specs=[
            pl.BlockSpec((levels, levels, chunk), lambda i: (0, 0, i)),
            pl.BlockSpec((values, chunk), lambda i: (0, i)),
        ],
        out_specs=pl.BlockSpec((values, chunk), lambda i: (0, i)),
        out_shape=jax.ShapeDtypeStruct((values, columns), F32),
        scratch_shapes=[pltpu.VMEM((values, chunk), F32)],
        compiler_params=params(),
        cost_estimate=cost(2 * values * levels * columns, 16 << 20),
        name="grad_mixed",
    )(matrix, incoming)


def network_kernel(
    arrived_ref, gm_ref, w_in_ref, w_out_t_ref, w_in_t_ref,
    leaving_ref, cols_ref, act_ref, wide, acc_in, acc_out, *, steps, tiles,
):
    step = pl.program_id(0)
    sources, rows = arrived_ref.shape[0], arrived_ref.shape[2]
    fields = rows // QROWS
    group = sources // tiles

    @pl.when(step == 0)
    def _():
        acc_in[...] = jnp.zeros_like(acc_in)
        acc_out[...] = jnp.zeros_like(acc_out)

    @pl.when(step < steps)
    def _():
        wide[...] = arrived_ref[:, 0].astype(F32).reshape(sources * rows, LANES)
        for q in range(QROWS):
            by_field = [wide[pl.ds(f * QROWS + q, sources, stride=rows), :] for f in range(fields)]
            parts = [
                by_field[f][a * group : (a + 1) * group] for a in range(tiles) for f in range(fields)
            ]
            cols_ref[:, q * LANES : (q + 1) * LANES] = jnp.concatenate(parts, axis=0).astype(BF)
        width = 256
        for j in range(QROWS * LANES // width):
            lanes = slice(j * width, (j + 1) * width)
            cols = cols_ref[:, lanes]
            pre = dot(w_in_ref[...], cols)
            sig = 0.5 + 0.5 * jnp.tanh(0.5 * pre)
            act = pre * sig
            act_b = act.astype(BF)
            act_ref[:, lanes] = act_b
            gm = gm_ref[:, lanes]
            gm_b = gm.astype(BF)
            grad_act = dot(w_out_t_ref[...], gm_b)
            grad_pre = (grad_act * (sig + act * (1.0 - sig))).astype(BF)
            grad_cols = gm + dot(w_in_t_ref[...], grad_pre)
            for k in range(width // LANES):
                q = j * (width // LANES) + k
                piece = grad_cols[:, k * LANES : (k + 1) * LANES]
                for f in range(fields):
                    parts = [
                        piece[(a * fields + f) * group : (a * fields + f + 1) * group]
                        for a in range(tiles)
                    ]
                    wide[pl.ds(f * QROWS + q, sources, stride=rows), :] = jnp.concatenate(parts, axis=0)
            acc_in[...] += dot(grad_pre, cols, (1, 1))
            acc_out[...] += dot(gm_b, act_b, (1, 1))
        leaving_ref[:, 0] = wide[...].reshape(sources, rows, LANES).astype(BF)

    @pl.when(step == steps)
    def _():
        place = 0
        for acc in (acc_in, acc_out):
            height, breadth = acc.shape
            for j in range(breadth // LANES):
                count = height // rows
                part = acc[:, j * LANES : (j + 1) * LANES].reshape(count, rows, LANES)
                leaving_ref[place : place + count, 0] = part.astype(BF)
                place += count


def network(arrived, grad_mixed, w_in, w_out_t, w_in_t, tiles):
    sources, steps, rows, _ = arrived.shape
    values, columns = grad_mixed.shape
    neurons = w_in.shape[0]
    chunk = columns // steps
    last = steps - 1
    whole = lambda i: (0, 0)
    return pl.pallas_call(
        functools.partial(network_kernel, steps=steps, tiles=tiles),
        grid=(steps + 1,),
        in_specs=[
            pl.BlockSpec((sources, 1, rows, LANES), lambda i: (0, jnp.minimum(i, last), 0, 0)),
            pl.BlockSpec((values, chunk), lambda i: (0, jnp.minimum(i, last))),
            pl.BlockSpec((neurons, values), whole),
            pl.BlockSpec((neurons, values), whole),
            pl.BlockSpec((values, neurons), whole),
        ],
        out_specs=[
            pl.BlockSpec((sources, 1, rows, LANES), lambda i: (0, i, 0, 0)),
            pl.BlockSpec((values, chunk), lambda i: (0, jnp.minimum(i, last))),
            pl.BlockSpec((neurons, chunk), lambda i: (0, jnp.minimum(i, last))),
        ],
        out_shape=[
            jax.ShapeDtypeStruct((sources, steps + 1, rows, LANES), BF),
            jax.ShapeDtypeStruct((values, columns), BF),
            jax.ShapeDtypeStruct((neurons, columns), BF),
        ],
        scratch_shapes=[
            pltpu.VMEM((sources * rows, LANES), F32),
            pltpu.VMEM((neurons, values), F32),
            pltpu.VMEM((values, neurons), F32),
        ],
        compiler_params=params(),
        cost_estimate=cost(10 * neurons * values * columns, 16 << 20, neurons * columns),
        name="column_network",
    )(arrived, grad_mixed, w_in, w_out_t, w_in_t)


def diffused_kernel(cols_ref, act_ref, w_out_ref, inv_ref, out_ref, mixed, flat):
    fields, levels = out_ref.shape[0], out_ref.shape[1]
    total = cols_ref[...].astype(F32) + dot(w_out_ref[...], act_ref[...])
    mixed[...] = total.astype(BF).astype(F32)

    def tile(t, carry):
        lanes = pl.ds(pl.multiple_of(t * LANES, LANES), LANES)
        flat[...] = inv_ref[:, :, lanes].astype(F32).reshape(levels * levels, LANES)
        acc = [None] * fields
        for m in range(levels):
            matrix = flat[pl.ds(m, levels, stride=levels), :]
            for f in range(fields):
                term = matrix * mixed[pl.ds(f * levels + m, 1), lanes]
                acc[f] = term if acc[f] is None else acc[f] + term
        for f in range(fields):
            out_ref[f, :, lanes] = acc[f]
        return carry

    lax.fori_loop(0, inv_ref.shape[2] // LANES, tile, 0)


def diffused_of(cols, act, w_out, matrix, fields):
    levels, _, columns = matrix.shape
    values, neurons = w_out.shape
    chunk = 512
    return pl.pallas_call(
        diffused_kernel,
        grid=(columns // chunk,),
        in_specs=[
            pl.BlockSpec((values, chunk), lambda i: (0, i)),
            pl.BlockSpec((neurons, chunk), lambda i: (0, i)),
            pl.BlockSpec((values, neurons), lambda i: (0, 0)),
            pl.BlockSpec((levels, levels, chunk), lambda i: (0, 0, i)),
        ],
        out_specs=pl.BlockSpec((fields, levels, chunk), lambda i: (0, 0, i)),
        out_shape=jax.ShapeDtypeStruct((fields, levels, columns), F32),
        scratch_shapes=[
            pltpu.VMEM((values, chunk), F32),
            pltpu.VMEM((levels * levels, LANES), F32),
        ],
        compiler_params=params(),
        cost_estimate=cost(2 * values * (levels + neurons) * columns, 20 << 20),
        name="diffused",
    )(cols, act, w_out, matrix)


def adjoint_kernel(back_ref, op_ref, out_ref, grid_ref, *, block):
    step = pl.program_id(0)
    fields = out_ref.shape[0]
    tiles, lon_tiles, chunks = back_ref.shape[:3]

    @pl.when(step == 0)
    def _():
        for a in range(tiles):
            wide = back_ref[a].astype(F32).reshape(lon_tiles * chunks, fields, QROWS, LANES)
            for f in range(fields):
                grid_ref[f, :, a * LANES : (a + 1) * LANES] = (
                    wide[:, f].reshape(lon_tiles * chunks * QROWS, LANES).astype(BF)
                )

    rows = pl.ds(pl.multiple_of(step * block, block), block)
    for f in range(fields):
        along = dot(op_ref[...], grid_ref[f])
        wide = grid_ref[f, rows, :].astype(F32)
        out_ref[f] = wide + along + KAPPA * meridional(wide)


def adjoint(returned, operator, fields, grid_lat):
    tiles, lon_tiles, _, rows, _ = returned.shape
    grid_lon = operator.shape[0]
    chunks = grid_lon // (lon_tiles * QROWS)
    block = 256
    return pl.pallas_call(
        functools.partial(adjoint_kernel, block=block),
        grid=(grid_lon // block,),
        in_specs=[
            pl.BlockSpec((tiles, lon_tiles, chunks, rows, LANES), lambda i: (0, 0, 0, 0, 0)),
            pl.BlockSpec((block, grid_lon), lambda i: (i, 0)),
        ],
        out_specs=pl.BlockSpec((fields, block, grid_lat), lambda i: (0, i, 0)),
        out_shape=jax.ShapeDtypeStruct((fields, grid_lon, grid_lat), F32),
        scratch_shapes=[pltpu.VMEM((fields, grid_lon, grid_lat), BF)],
        compiler_params=params(),
        cost_estimate=cost(2 * fields * grid_lon * grid_lon * grid_lat, 8 << 20),
        name="adjoint_dynamics",
    )(returned, operator)


def weight_sum_kernel(parts_ref, _, out_ref):
    total = jnp.sum(parts_ref[:, 0].astype(F32), axis=0, keepdims=True)
    out_ref[...] = jnp.broadcast_to(total.astype(BF), out_ref.shape)


def weight_sum(returned, after):
    sources, chunks, rows, _ = returned.shape
    return pl.pallas_call(
        weight_sum_kernel,
        grid=(1,),
        in_specs=[
            pl.BlockSpec((sources, 1, rows, LANES), lambda i: (0, chunks - 1, 0, 0)),
            pl.BlockSpec(memory_space=pl.ANY),
        ],
        out_specs=pl.BlockSpec((sources, rows, LANES), lambda i: (0, 0, 0)),
        out_shape=jax.ShapeDtypeStruct((sources, rows, LANES), BF),
        compiler_params=params(),
        cost_estimate=cost(sources * rows * LANES, 1 << 20),
        name="weight_sum",
    )(returned, after)


def weight_spread_kernel(shares_ref, in_ref, out_ref):
    rows = shares_ref.shape[1]
    place = 0
    for ref in (in_ref, out_ref):
        height, breadth = ref.shape
        for j in range(breadth // LANES):
            count = height // rows
            part = shares_ref[place : place + count].astype(F32)
            ref[:, j * LANES : (j + 1) * LANES] = part.reshape(height, LANES)
            place += count


def weight_spread(shares, neurons, values):
    return pl.pallas_call(
        weight_spread_kernel,
        out_shape=[
            jax.ShapeDtypeStruct((neurons, values), F32),
            jax.ShapeDtypeStruct((values, neurons), F32),
        ],
        compiler_params=params(),
        name="weight_spread",
    )(shares)


def exchange(array):
    return lax.all_to_all(array, AXES, split_axis=0, concat_axis=0, tiled=True)


def per_device(fields_in, lon_operator, w_in, w_out, inverses, cotangent):
    lat_tiles = lax.axis_size("lat")
    lon_tiles = lax.axis_size("lon")
    devices = lat_tiles * lon_tiles
    field_dev, _, grid_lon, grid_lat = fields_in.shape
    all_fields, all_levels, columns = cotangent.shape[2:]
    neurons, values = w_in.shape
    tile_lon = grid_lon // lon_tiles

    leaving = forward(
        fields_in.reshape(field_dev, grid_lon, grid_lat), lon_operator, lat_tiles, lon_tiles, tile_lon
    )
    arrived = exchange(leaving.reshape((devices,) + leaving.shape[2:]))

    matrix = inverses.reshape(all_levels, all_levels, columns)
    grad_mixed = grad_mixed_of(matrix, cotangent.reshape(values, columns))

    going, cols, act = network(arrived, grad_mixed, w_in, w_out.T, w_in.T, lat_tiles)
    returned = exchange(going)

    diffused = diffused_of(cols, act, w_out, matrix, all_fields)

    shares = exchange(weight_sum(returned, diffused))
    grad_fields = adjoint(
        returned.reshape((lat_tiles, lon_tiles) + returned.shape[1:]), lon_operator, field_dev, grid_lat
    )
    grad_in, grad_out = weight_spread(shares, neurons, values)
    return (
        diffused.reshape(1, 1, all_fields, all_levels, columns),
        grad_fields.reshape(field_dev, 1, grid_lon, grid_lat),
        grad_in,
        grad_out,
    )


def solution(mesh):
    in_specs = (
        P("lat", "lon", None, None),
        P(),
        P(),
        P(),
        P("lat", "lon", None, None, None),
        P("lat", "lon", None, None, None),
    )
    out_specs = (P("lat", "lon", None, None, None), P("lat", "lon", None, None), P(), P())
    return jax.shard_map(
        per_device, mesh=mesh, in_specs=in_specs, out_specs=out_specs, check_vma=False
    )
```

profile of v0, /device:TPU:1, one launch (start us, length us, event | category | flops | bytes accessed | tf_op | source)
XLA Modules:
  0.0 127.8 jit_solution(7987549032472800793)
XLA Ops:
  0.6 6.6 %forward_dynamics.1 = bf16[4,32,4,16,128]{4,3,2,1,0:T(8,128)(2,1)} custom-call(bf16[2,1024,512]{2,1,0:T(8,128)(2,1)} %bitcast.20, bf16[1024,1024]{1,0:T(8,128)(2,1)} %op_ref.3), custom_call_target="tpu_custom_call" | custom-call | flops 2147483648 | bytes 6291456 | tf_op jit(solution)/shard_map/forward_dynamics/pallas_call | solution.py:62
  7.2 0.0 copy-start.4
  7.2 0.0 copy-start.3
  7.2 11.5 %all-to-all-start = ((bf16[128,4,16,128]{3,2,1,0:T(8,128)(2,1)}), bf16[128,4,16,128]{3,2,1,0:T(8,128)(2,1)S(1)}, u32[]{:S(2)}, u32[]{:S(2)}) async-start(bf16[128,4,16,128]{3,2,1,0:T(8,128)(2,1)} %bitcast.17), calls=%async_computation | async-start | bytes 4194304 | tf_op jit(solution)/shard_map/all_to_all | solution.py:354
  18.7 0.0 copy-done.4
  18.7 0.8 copy.11
  19.6 0.0 copy-done.3
  19.6 0.8 copy.10
  20.4 13.5 %grad_mixed.1.gm_ref = f32[256,4096]{1,0:T(8,128)} custom-call(bf16[32,32,4096]{2,1,0:T(8,128)(2,1)} %bitcast.11, bf16[256,4096]{1,0:T(8,128)(2,1)} %bitcast.16), custom_call_target="tpu_custom_call" | custom-call | flops 67108864 | bytes 16777216 | tf_op jit(solution)/shard_map/grad_mixed/pallas_call | solution.py:103
  33.9 15.3 %all-to-all-done.arrived_ref = bf16[128,4,16,128]{3,2,1,0:T(8,128)(2,1)S(1)} async-done(((bf16[128,4,16,128]{3,2,1,0:T(8,128)(2,1)}), bf16[128,4,16,128]{3,2,1,0:T(8,128)(2,1)S(1)}, u32[]{:S(2)}, u32[]{:S(2)}) %all-to-all-start) | async-done | bytes 2097184 | tf_op jit(solution)/shard_map/all_to_all | solution.py:354
  49.2 0.0 copy-start.1
  49.2 1.3 %copy-done.1 = bf16[128,4,16,128]{3,2,1,0:T(8,128)(2,1)} copy-done((bf16[128,4,16,128]{3,2,1,0:T(8,128)(2,1)}, bf16[128,4,16,128]{3,2,1,0:T(8,128)(2,1)S(1)}, u32[]{:S(2)}) %copy-start.1) | copy-done | bytes 2097176
  50.5 12.9 %column_network.1 = (bf16[128,5,16,128]{3,2,1,0:T(8,128)(2,1)}, bf16[256,4096]{1,0:T(8,128)(2,1)}, bf16[512,4096]{1,0:T(8,128)(2,1)}) custom-call(bf16[128,4,16,128]{3,2,1,0:T(8,128)(2,1)} %copy-done.1, f32[256,4096]{1,0:T(8,128)} %grad_mixed.1.gm_ref, bf16[512,256]{1,0:T(8,128)(2,1)} %w_in_ref.1, bf16[512,256]{1,0:T(8,128)(2,1)} %bitcast.19, ...), custom_call_target="tpu_custom_call" | custom-call | flops 5368709120 | bytes 16777216 | tf_op jit(solution)/shard_map/column_network/pallas_call | solution.py:188
  63.4 4.0 %all-to-all-start.1 = ((bf16[128,5,16,128]{3,2,1,0:T(8,128)(2,1)}), bf16[128,5,16,128]{3,2,1,0:T(8,128)(2,1)S(1)}, u32[]{:S(2)}, u32[]{:S(2)}) async-start(bf16[128,5,16,128]{3,2,1,0:T(8,128)(2,1)} %get-tuple-element.11), calls=%async_computation.1 | async-start | bytes 5242880 | tf_op jit(solution)/shard_map/all_to_all | solution.py:354
  67.4 22.2 %diffused.1._ = f32[8,32,4096]{2,1,0:T(8,128)} custom-call(bf16[256,4096]{1,0:T(8,128)(2,1)} %get-tuple-element.9.cols_ref, bf16[512,4096]{1,0:T(8,128)(2,1)} %get-tuple-element.10.act_ref, bf16[256,512]{1,0:T(8,128)(2,1)} %w_out_ref.1, bf16[32,32,4096]{2,1,0:T(8,128)(2,1)} %bitcast.12), custom_call_target="tpu_custom_call" | custom-call | flops 1140850688 | bytes 20971520 | tf_op jit(solution)/shard_map/diffused/pallas_call | solution.py:244
  89.6 13.9 %all-to-all-done.1.parts_ref = bf16[128,5,16,128]{3,2,1,0:T(8,128)(2,1)S(1)} async-done(((bf16[128,5,16,128]{3,2,1,0:T(8,128)(2,1)}), bf16[128,5,16,128]{3,2,1,0:T(8,128)(2,1)S(1)}, u32[]{:S(2)}, u32[]{:S(2)}) %all-to-all-start.1) | async-done | bytes 2621472 | tf_op jit(solution)/shard_map/all_to_all | solution.py:354
  103.5 1.5 %copy-done = bf16[128,5,16,128]{3,2,1,0:T(8,128)(2,1)} copy-done((bf16[128,5,16,128]{3,2,1,0:T(8,128)(2,1)}, bf16[128,5,16,128]{3,2,1,0:T(8,128)(2,1)S(1)}, u32[]{:S(2)}) %copy-start) | copy-done | bytes 2621464
  105.0 2.0 %weight_sum.1 = bf16[128,16,128]{2,1,0:T(8,128)(2,1)} custom-call(bf16[128,5,16,128]{3,2,1,0:T(8,128)(2,1)} %copy-done, f32[8,32,4096]{2,1,0:T(8,128)} %diffused.1._), custom_call_target="tpu_custom_call" | custom-call | flops 262144 | bytes 1048576 | tf_op jit(solution)/shard_map/weight_sum/pallas_call | solution.py:314
  107.0 4.1 %all-to-all-start.2 = ((bf16[128,16,128]{2,1,0:T(8,128)(2,1)}), bf16[128,16,128]{2,1,0:T(8,128)(2,1)S(1)}, u32[]{:S(2)}, u32[]{:S(2)}) async-start(bf16[128,16,128]{2,1,0:T(8,128)(2,1)} %weight_sum.1), calls=%async_computation.2 | async-start | bytes 1048576 | tf_op jit(solution)/shard_map/all_to_all | solution.py:354
  111.2 7.3 %adjoint_dynamics.1 = f32[2,1024,512]{2,1,0:T(8,128)} custom-call(bf16[4,32,5,16,128]{4,3,2,1,0:T(8,128)(2,1)} %bitcast.13, bf16[1024,1024]{1,0:T(8,128)(2,1)} %op_ref.3), custom_call_target="tpu_custom_call" | custom-call | flops 2147483648 | bytes 8388608 | tf_op jit(solution)/shard_map/adjoint_dynamics/pallas_call | solution.py:291
  118.5 6.5 %all-to-all-done.2.shares_ref = bf16[128,16,128]{2,1,0:T(8,128)(2,1)S(1)} async-done(((bf16[128,16,128]{2,1,0:T(8,128)(2,1)}), bf16[128,16,128]{2,1,0:T(8,128)(2,1)S(1)}, u32[]{:S(2)}, u32[]{:S(2)}) %all-to-all-start.2) | async-done | bytes 524320 | tf_op jit(solution)/shard_map/all_to_all | solution.py:354
  125.0 0.0 copy-start.2
  125.0 0.8 copy-done.2
  125.8 2.0 %weight_spread.1 = (f32[512,256]{1,0:T(8,128)}, f32[256,512]{1,0:T(8,128)}) custom-call(bf16[128,16,128]{2,1,0:T(8,128)(2,1)} %copy-done.2), custom_call_target="tpu_custom_call" | custom-call | tf_op jit(solution)/shard_map/weight_spread/pallas_call | solution.py:342
  (1 shorter events, 0.0 us)
Async XLA Ops:
  7.2 11.5 %copy-start.4 = (bf16[512,256]{1,0:T(8,128)(2,1)S(1)}, bf16[512,256]{1,0:T(8,128)(2,1)}, u32[]{:S(2)}) copy-start(bf16[512,256]{1,0:T(8,128)(2,1)} %w_in_ref.1) | copy-start | bytes 786436
  7.2 12.4 %copy-start.3 = (bf16[256,512]{1,0:T(8,128)(2,1)S(1)}, bf16[256,512]{1,0:T(8,128)(2,1)}, u32[]{:S(2)}) copy-start(bf16[256,512]{1,0:T(8,128)(2,1)} %w_out_ref.1) | copy-start | bytes 786436
  7.2 42.0 %all-to-all-start = ((bf16[128,4,16,128]{3,2,1,0:T(8,128)(2,1)}), bf16[128,4,16,128]{3,2,1,0:T(8,128)(2,1)S(1)}, u32[]{:S(2)}, u32[]{:S(2)}) async-start(bf16[128,4,16,128]{3,2,1,0:T(8,128)(2,1)} %bitcast.17), calls=%async_computation | async-start | bytes 4194304 | tf_op jit(solution)/shard_map/all_to_all | solution.py:354
  49.2 1.3 %copy-start.1 = (bf16[128,4,16,128]{3,2,1,0:T(8,128)(2,1)}, bf16[128,4,16,128]{3,2,1,0:T(8,128)(2,1)S(1)}, u32[]{:S(2)}) copy-start(bf16[128,4,16,128]{3,2,1,0:T(8,128)(2,1)S(1)} %all-to-all-done.arrived_ref) | copy-start | bytes 6291460
  63.4 40.1 %all-to-all-start.1 = ((bf16[128,5,16,128]{3,2,1,0:T(8,128)(2,1)}), bf16[128,5,16,128]{3,2,1,0:T(8,128)(2,1)S(1)}, u32[]{:S(2)}, u32[]{:S(2)}) async-start(bf16[128,5,16,128]{3,2,1,0:T(8,128)(2,1)} %get-tuple-element.11), calls=%async_computation.1 | async-start | bytes 5242880 | tf_op jit(solution)/shard_map/all_to_all | solution.py:354
  103.5 1.5 %copy-start = (bf16[128,5,16,128]{3,2,1,0:T(8,128)(2,1)}, bf16[128,5,16,128]{3,2,1,0:T(8,128)(2,1)S(1)}, u32[]{:S(2)}) copy-start(bf16[128,5,16,128]{3,2,1,0:T(8,128)(2,1)S(1)} %all-to-all-done.1.parts_ref) | copy-start | bytes 7864324
  107.0 17.9 %all-to-all-start.2 = ((bf16[128,16,128]{2,1,0:T(8,128)(2,1)}), bf16[128,16,128]{2,1,0:T(8,128)(2,1)S(1)}, u32[]{:S(2)}, u32[]{:S(2)}) async-start(bf16[128,16,128]{2,1,0:T(8,128)(2,1)} %weight_sum.1), calls=%async_computation.2 | async-start | bytes 1048576 | tf_op jit(solution)/shard_map/all_to_all | solution.py:354
  125.0 0.8 copy-start.2
where the time goes:
time: 129 us; the launch traced here: 128 us
  Pallas kernels  66.6 us (52%)
  waiting for transfers between devices  35.7 us (28%)
  starting transfers between devices  19.6 us (15%)
  local copies, waits for them, and re-layouts  5.33 us (4%)
    all_to_all x3, waiting for transfers between devices, exchange(): return lax.all_to_all(array, AXES, split_axis=0, concat_axis=0, tiled=True)  35.7 us
    pallas_call x1, Pallas kernels, diffused_of(): pl.pallas_call(diffused_kernel, grid=(columns // chunk,), in_specs=[pl.Bl...  22.2 us
    all_to_all x3, starting transfers between devices, exchange(): return lax.all_to_all(array, AXES, split_axis=0, concat_axis=0, tiled=True)  19.6 us
    pallas_call x1, Pallas kernels, grad_mixed_of(): pl.pallas_call(grad_mixed_kernel, grid=(columns // chunk,), in_specs=[pl....  13.5 us
    pallas_call x1, Pallas kernels, network(): pl.pallas_call(functools.partial(network_kernel, steps=steps, tiles=tiles...  12.9 us
    pallas_call x1, Pallas kernels, adjoint(): pl.pallas_call(functools.partial(adjoint_kernel, block=block), grid=(grid...  7.29 us
    pallas_call x1, Pallas kernels, forward(): pl.pallas_call(functools.partial(forward_kernel, block=block), grid=(grid...  6.57 us
    unnamed x12, local copies, waits for them, and re-layouts  5.33 us
  transfers between devices with their start and end apart: 3, of which 3 were waited for; matrix products, arithmetic and copies ran while one was open for 1% of the time, Pallas kernels for 34%

commit v1 on v0

v1 whole, which is shorter than its diff:
```python
import functools

import jax
import jax.numpy as jnp
from jax import lax
from jax.experimental import pallas as pl
from jax.experimental.pallas import tpu as pltpu
from jax.sharding import PartitionSpec as P

KAPPA = 0.2
AXES = ("lat", "lon")
BF = jnp.bfloat16
F32 = jnp.float32
LANES = 128
QROWS = 8
VMEM_LIMIT = 60 * 1024 * 1024


def params():
    return pltpu.CompilerParams(vmem_limit_bytes=VMEM_LIMIT)


def cost(flops, nbytes, trans=0):
    return pl.CostEstimate(flops=int(flops), bytes_accessed=int(nbytes), transcendentals=int(trans))


def dot(a, b, dims=(1, 0)):
    return lax.dot_general(a, b, (((dims[0],), (dims[1],)), ((), ())), preferred_element_type=F32)


def spread(wide):
    size = wide.shape[1]
    lane = lax.broadcasted_iota(jnp.int32, wide.shape, 1)
    before = jnp.where(lane == 0, 0.0, pltpu.roll(wide, 1, 1))
    after = jnp.where(lane == size - 1, 0.0, pltpu.roll(wide, size - 1, 1))
    return (1.0 - 2.0 * KAPPA) * wide + KAPPA * (after + before)


def forward_kernel(v_hbm, op_hbm, out_hbm, v_ref, op_ref, out_ref, v_sem, op_sem, out_sem):
    fields = v_ref.shape[0]
    blocks = op_ref.shape[0]
    block = op_ref.shape[2]
    tiles, _, chunks, rows, _ = out_ref.shape
    tile_lon = chunks * QROWS
    per_block = block // tile_lon

    def fetch_op(i):
        return pltpu.make_async_copy(op_hbm.at[:, pl.ds(i * block, block)], op_ref.at[i], op_sem.at[i])

    def fetch_v(f):
        return pltpu.make_async_copy(v_hbm.at[f], v_ref.at[f], v_sem.at[f])

    def store(i):
        part = pl.ds(i * per_block, per_block)
        return pltpu.make_async_copy(out_ref.at[:, part], out_hbm.at[:, part], out_sem.at[i])

    fetch_op(0).start()
    for f in range(fields):
        fetch_v(f).start()
    for i in range(1, blocks):
        fetch_op(i).start()
    def step(i, carry):
        fetch_op(i).wait()

        @pl.when(i == 0)
        def _():
            for f in range(fields):
                fetch_v(f).wait()

        rows_here = pl.ds(pl.multiple_of(i * block, block), block)
        done = []
        for f in range(fields):
            along = dot(op_ref[i], v_ref[f], (0, 0))
            wide = v_ref[f, rows_here, :].astype(F32)
            done.append(along + spread(wide))
        for a in range(tiles):
            parts = [
                d[:, a * LANES : (a + 1) * LANES].reshape(per_block, chunks, 1, QROWS, LANES)
                for d in done
            ]
            joined = jnp.concatenate(parts, axis=2).reshape(per_block, chunks, rows, LANES)
            out_ref[a, pl.ds(i * per_block, per_block)] = joined.astype(BF)
        store(i).start()
        return carry

    lax.fori_loop(0, blocks, step, 0)
    for i in range(blocks):
        store(i).wait()


def forward(fields_in, operator, lat_tiles, lon_tiles, tile_lon):
    fields, grid_lon, grid_lat = fields_in.shape
    chunks = tile_lon // QROWS
    block = 256
    blocks = grid_lon // block
    out_shape = (lat_tiles, lon_tiles, chunks, fields * QROWS, LANES)
    return pl.pallas_call(
        forward_kernel,
        in_specs=[pl.BlockSpec(memory_space=pltpu.HBM)] * 2,
        out_specs=pl.BlockSpec(memory_space=pltpu.HBM),
        out_shape=jax.ShapeDtypeStruct(out_shape, BF),
        scratch_shapes=[
            pltpu.VMEM(fields_in.shape, BF),
            pltpu.VMEM((blocks, grid_lon, block), BF),
            pltpu.VMEM(out_shape, BF),
            pltpu.SemaphoreType.DMA((fields,)),
            pltpu.SemaphoreType.DMA((blocks,)),
            pltpu.SemaphoreType.DMA((blocks,)),
        ],
        compiler_params=params(),
        cost_estimate=cost(2 * fields * grid_lon * grid_lon * grid_lat, 6 << 20),
        name="forward_dynamics",
    )(fields_in, operator)


def grad_mixed_kernel(inv_ref, cot_ref, out_ref, wide):
    levels = inv_ref.shape[0]
    fields = cot_ref.shape[0] // levels
    wide[...] = cot_ref[...].astype(F32)

    def tile(t, carry):
        lanes = pl.ds(pl.multiple_of(t * LANES, LANES), LANES)
        acc = [None] * fields
        for l in range(levels):
            matrix = inv_ref[l, :, lanes].astype(F32)
            for f in range(fields):
                term = matrix * wide[pl.ds(f * levels + l, 1), lanes]
                acc[f] = term if acc[f] is None else acc[f] + term
        for f in range(fields):
            out_ref[f * levels : (f + 1) * levels, lanes] = acc[f].astype(BF)
        return carry

    lax.fori_loop(0, inv_ref.shape[2] // LANES, tile, 0)


def grad_mixed_of(matrix, incoming):
    levels, _, columns = matrix.shape
    values = incoming.shape[0]
    chunk = 512
    return pl.pallas_call(
        grad_mixed_kernel,
        grid=(columns // chunk,),
        in_specs=[
            pl.BlockSpec((levels, levels, chunk), lambda i: (0, 0, i)),
            pl.BlockSpec((values, chunk), lambda i: (0, i)),
        ],
        out_specs=pl.BlockSpec((values, chunk), lambda i: (0, i)),
        out_shape=jax.ShapeDtypeStruct((values, columns), BF),
        scratch_shapes=[pltpu.VMEM((values, chunk), F32)],
        compiler_params=params(),
        cost_estimate=cost(2 * values * levels * columns, 16 << 20),
        name="grad_mixed",
    )(matrix, incoming)


def network_kernel(
    arrived_hbm, gm_hbm, w_half_hbm, w_out_hbm,
    leaving_hbm, cols_hbm,
    arrived, gm, w_half, w_out, leaving, cols, act, grad_pre, wide_in, wide_out, acc_in, acc_out,
    in_sem, w_sem, out_sem, *, tiles,
):
    sources, steps, rows, _ = arrived_hbm.shape
    fields = rows // QROWS
    group = sources // tiles
    chunk = QROWS * LANES

    def fetch(i):
        lanes = pl.ds(i * chunk, chunk)
        return (
            pltpu.make_async_copy(arrived_hbm.at[:, i], arrived.at[i], in_sem.at[0, i]),
            pltpu.make_async_copy(gm_hbm.at[:, lanes], gm.at[i], in_sem.at[1, i]),
        )

    def fetch_weights():
        return [
            pltpu.make_async_copy(w_half_hbm, w_half, w_sem.at[0]),
            pltpu.make_async_copy(w_out_hbm, w_out, w_sem.at[1]),
        ]

    def store_leaving(i):
        return pltpu.make_async_copy(leaving.at[i], leaving_hbm.at[:, i], out_sem.at[0, i])

    def store_cols(i):
        return pltpu.make_async_copy(
            cols.at[i], cols_hbm.at[:, pl.ds(i * chunk, chunk)], out_sem.at[1, i]
        )

    weights = fetch_weights()
    first = fetch(0)
    first[0].start()
    weights[0].start()
    first[1].start()
    weights[1].start()
    for i in range(1, steps):
        for copy in fetch(i):
            copy.start()
    acc_in[...] = jnp.zeros_like(acc_in)
    acc_out[...] = jnp.zeros_like(acc_out)
    for copy in weights:
        copy.wait()

    def step(i, carry):
        for copy in fetch(i):
            copy.wait()
        wide_in[...] = arrived[i].astype(F32).reshape(sources * rows, LANES)
        for q in range(QROWS):
            by_field = [
                wide_in[pl.ds(f * QROWS + q, sources, stride=rows), :] for f in range(fields)
            ]
            parts = [
                by_field[f][a * group : (a + 1) * group] for a in range(tiles) for f in range(fields)
            ]
            cols[i, :, q * LANES : (q + 1) * LANES] = jnp.concatenate(parts, axis=0).astype(BF)
        half = dot(w_half[...], cols[i])
        turn = jnp.tanh(half)
        value = half + half * turn
        act[...] = value.astype(BF)
        slope = 1.0 + (turn + value) - turn * value
        grad_pre[...] = (dot(w_out[...], gm[i], (0, 0)) * slope).astype(BF)
        grad_cols = gm[i].astype(F32) + dot(w_half[...], grad_pre[...], (0, 0))
        acc_in[...] += dot(grad_pre[...], cols[i], (1, 1))
        acc_out[...] += dot(act[...], gm[i], (1, 1))
        for q in range(QROWS):
            piece = grad_cols[:, q * LANES : (q + 1) * LANES]
            for f in range(fields):
                parts = [
                    piece[(a * fields + f) * group : (a * fields + f + 1) * group]
                    for a in range(tiles)
                ]
                wide_out[pl.ds(f * QROWS + q, sources, stride=rows), :] = jnp.concatenate(
                    parts, axis=0
                )
        leaving[i] = wide_out[...].reshape(sources, rows, LANES).astype(BF)
        store_cols(i).start()
        store_leaving(i).start()
        return carry

    lax.fori_loop(0, steps, step, 0)
    total_in = 0.5 * acc_in[...]
    total_out = acc_out[...]
    place = 0
    for total in (total_in, total_out):
        height, breadth = total.shape
        for j in range(breadth // LANES):
            count = height // rows
            part = total[:, j * LANES : (j + 1) * LANES].reshape(count, rows, LANES)
            leaving[steps, place : place + count] = part.astype(BF)
            place += count
    store_leaving(steps).start()
    for i in range(steps):
        store_cols(i).wait()
        store_leaving(i).wait()
    store_leaving(steps).wait()


def network(arrived, grad_mixed, w_half, w_out, tiles):
    sources, steps, rows, _ = arrived.shape
    values, columns = grad_mixed.shape
    neurons = w_half.shape[0]
    chunk = columns // steps
    return pl.pallas_call(
        functools.partial(network_kernel, tiles=tiles),
        in_specs=[pl.BlockSpec(memory_space=pltpu.HBM)] * 4,
        out_specs=[pl.BlockSpec(memory_space=pltpu.HBM)] * 2,
        out_shape=[
            jax.ShapeDtypeStruct((sources, steps + 1, rows, LANES), BF),
            jax.ShapeDtypeStruct((values, columns), BF),
        ],
        scratch_shapes=[
            pltpu.VMEM((steps, sources, rows, LANES), BF),
            pltpu.VMEM((steps, values, chunk), BF),
            pltpu.VMEM((neurons, values), BF),
            pltpu.VMEM((values, neurons), BF),
            pltpu.VMEM((steps + 1, sources, rows, LANES), BF),
            pltpu.VMEM((steps, values, chunk), BF),
            pltpu.VMEM((neurons, chunk), BF),
            pltpu.VMEM((neurons, chunk), BF),
            pltpu.VMEM((sources * rows, LANES), F32),
            pltpu.VMEM((sources * rows, LANES), F32),
            pltpu.VMEM((neurons, values), F32),
            pltpu.VMEM((neurons, values), F32),
            pltpu.SemaphoreType.DMA((2, steps)),
            pltpu.SemaphoreType.DMA((2,)),
            pltpu.SemaphoreType.DMA((2, steps + 1)),
        ],
        compiler_params=params(),
        cost_estimate=cost(8 * neurons * values * columns, 14 << 20, neurons * columns),
        name="column_network",
    )(arrived, grad_mixed, w_half, w_out)


def diffused_kernel(cols_ref, w_half_ref, w_out_ref, inv_ref, out_ref, mixed, flat):
    fields, levels = out_ref.shape[0], out_ref.shape[1]
    half = dot(w_half_ref[...], cols_ref[...])
    act = (half + half * jnp.tanh(half)).astype(BF)
    total = cols_ref[...].astype(F32) + dot(w_out_ref[...], act)
    mixed[...] = total.astype(BF).astype(F32)

    def tile(t, carry):
        lanes = pl.ds(pl.multiple_of(t * LANES, LANES), LANES)
        flat[...] = inv_ref[:, :, lanes].astype(F32).reshape(levels * levels, LANES)
        acc = [None] * fields
        for m in range(levels):
            matrix = flat[pl.ds(m, levels, stride=levels), :]
            for f in range(fields):
                term = matrix * mixed[pl.ds(f * levels + m, 1), lanes]
                acc[f] = term if acc[f] is None else acc[f] + term
        for f in range(fields):
            out_ref[f, :, lanes] = acc[f]
        return carry

    lax.fori_loop(0, inv_ref.shape[2] // LANES, tile, 0)


def diffused_of(cols, w_half, w_out, matrix, fields):
    levels, _, columns = matrix.shape
    values, neurons = w_out.shape
    chunk = 512
    return pl.pallas_call(
        diffused_kernel,
        grid=(columns // chunk,),
        in_specs=[
            pl.BlockSpec((values, chunk), lambda i: (0, i)),
            pl.BlockSpec((neurons, values), lambda i: (0, 0)),
            pl.BlockSpec((values, neurons), lambda i: (0, 0)),
            pl.BlockSpec((levels, levels, chunk), lambda i: (0, 0, i)),
        ],
        out_specs=pl.BlockSpec((fields, levels, chunk), lambda i: (0, 0, i)),
        out_shape=jax.ShapeDtypeStruct((fields, levels, columns), F32),
        scratch_shapes=[
            pltpu.VMEM((values, chunk), F32),
            pltpu.VMEM((levels * levels, LANES), F32),
        ],
        compiler_params=params(),
        cost_estimate=cost(2 * values * (levels + 2 * neurons) * columns, 16 << 20),
        name="diffused",
    )(cols, w_half, w_out, matrix)


def adjoint_kernel(back_hbm, op_hbm, out_hbm, back, op_ref, grid_ref, out_ref, back_sem, op_sem, out_sem):
    fields = out_ref.shape[0]
    tiles, lon_tiles, chunks, rows, _ = back.shape
    grid_lon = grid_ref.shape[1]
    block = 256
    blocks = grid_lon // block

    def fetch_back(a):
        return pltpu.make_async_copy(back_hbm.at[a, :, pl.ds(0, chunks)], back.at[a], back_sem.at[a])

    def fetch_op(i):
        part = pl.ds(i * block, block)
        return pltpu.make_async_copy(op_hbm.at[part], op_ref.at[part], op_sem.at[i])

    def store(f, i):
        part = pl.ds(i * block, block)
        return pltpu.make_async_copy(out_ref.at[f, part], out_hbm.at[f, part], out_sem.at[f, i])

    for a in range(tiles):
        fetch_back(a).start()
    for i in range(blocks):
        fetch_op(i).start()
    for a in range(tiles):
        fetch_back(a).wait()
        wide = back[a].astype(F32).reshape(lon_tiles * chunks, fields, QROWS, LANES)
        for f in range(fields):
            grid_ref[f, :, a * LANES : (a + 1) * LANES] = (
                wide[:, f].reshape(grid_lon, LANES).astype(BF)
            )
    def step(i, carry):
        fetch_op(i).wait()
        part = pl.ds(pl.multiple_of(i * block, block), block)
        for f in range(fields):
            along = dot(op_ref[part, :], grid_ref[f])
            wide = grid_ref[f, part, :].astype(F32)
            out_ref[f, part, :] = along + spread(wide)
            store(f, i).start()
        return carry

    lax.fori_loop(0, blocks, step, 0)
    for i in range(blocks):
        for f in range(fields):
            store(f, i).wait()


def adjoint(returned, operator, fields, grid_lat):
    tiles, lon_tiles, _, rows, _ = returned.shape
    grid_lon = operator.shape[0]
    chunks = grid_lon // (lon_tiles * QROWS)
    blocks = grid_lon // 256
    return pl.pallas_call(
        adjoint_kernel,
        in_specs=[pl.BlockSpec(memory_space=pltpu.HBM)] * 2,
        out_specs=pl.BlockSpec(memory_space=pltpu.HBM),
        out_shape=jax.ShapeDtypeStruct((fields, grid_lon, grid_lat), F32),
        scratch_shapes=[
            pltpu.VMEM((tiles, lon_tiles, chunks, rows, LANES), BF),
            pltpu.VMEM(operator.shape, BF),
            pltpu.VMEM((fields, grid_lon, grid_lat), BF),
            pltpu.VMEM((fields, grid_lon, grid_lat), F32),
            pltpu.SemaphoreType.DMA((tiles,)),
            pltpu.SemaphoreType.DMA((blocks,)),
            pltpu.SemaphoreType.DMA((fields, blocks)),
        ],
        compiler_params=params(),
        cost_estimate=cost(2 * fields * grid_lon * grid_lon * grid_lat, 8 << 20),
        name="adjoint_dynamics",
    )(returned, operator)


def weight_sum_kernel(returned_hbm, _, out_hbm, parts, out_ref, in_sem, out_sem):
    pieces = in_sem.shape[0]
    each = parts.shape[0] // pieces
    last = returned_hbm.shape[1] - 1

    def fetch(k):
        part = pl.ds(k * each, each)
        return pltpu.make_async_copy(returned_hbm.at[part, last], parts.at[part], in_sem.at[k])

    for k in range(pieces):
        fetch(k).start()
    total = None
    for k in range(pieces):
        fetch(k).wait()
        piece = jnp.sum(parts[k * each : (k + 1) * each].astype(F32), axis=0, keepdims=True)
        total = piece if total is None else total + piece
    out_ref[...] = jnp.broadcast_to(total.astype(BF), out_ref.shape)
    store = pltpu.make_async_copy(out_ref, out_hbm, out_sem)
    store.start()
    store.wait()


def weight_sum(returned, after):
    sources, _, rows, _ = returned.shape
    shape = (sources, rows, LANES)
    return pl.pallas_call(
        weight_sum_kernel,
        in_specs=[pl.BlockSpec(memory_space=pltpu.HBM)] * 2,
        out_specs=pl.BlockSpec(memory_space=pltpu.HBM),
        out_shape=jax.ShapeDtypeStruct(shape, BF),
        scratch_shapes=[
            pltpu.VMEM(shape, BF),
            pltpu.VMEM(shape, BF),
            pltpu.SemaphoreType.DMA((4,)),
            pltpu.SemaphoreType.DMA,
        ],
        compiler_params=params(),
        cost_estimate=cost(sources * rows * LANES, 1 << 20),
        name="weight_sum",
    )(returned, after)


def weight_spread_kernel(shares_hbm, in_hbm, out_hbm, shares, in_ref, out_ref, in_sem, out_sem):
    rows = shares.shape[1]
    height, breadth = in_ref.shape
    count = height // rows
    each = breadth // LANES
    jobs = 2 * each

    def fetch(k):
        part = pl.ds(k * count, count)
        return pltpu.make_async_copy(shares_hbm.at[part], shares.at[part], in_sem.at[k])

    def store(k):
        part = pl.ds((k % each) * LANES, LANES)
        if k < each:
            return pltpu.make_async_copy(in_ref.at[:, part], in_hbm.at[:, part], out_sem.at[k])
        return pltpu.make_async_copy(out_ref.at[part], out_hbm.at[part], out_sem.at[k])

    for k in range(jobs):
        fetch(k).start()
    for k in range(jobs):
        fetch(k).wait()
        wide = shares[k * count : (k + 1) * count].astype(F32).reshape(height, LANES)
        part = slice((k % each) * LANES, (k % each + 1) * LANES)
        if k < each:
            in_ref[:, part] = wide
        else:
            out_ref[part, :] = wide.T
        store(k).start()
    for k in range(jobs):
        store(k).wait()


def weight_spread(shares, neurons, values):
    shapes = [(neurons, values), (values, neurons)]
    jobs = 2 * (values // LANES)
    return pl.pallas_call(
        weight_spread_kernel,
        in_specs=[pl.BlockSpec(memory_space=pltpu.HBM)],
        out_specs=[pl.BlockSpec(memory_space=pltpu.HBM)] * 2,
        out_shape=[jax.ShapeDtypeStruct(shape, F32) for shape in shapes],
        scratch_shapes=[pltpu.VMEM(shares.shape, BF)]
        + [pltpu.VMEM(shape, F32) for shape in shapes]
        + [pltpu.SemaphoreType.DMA((jobs,))] * 2,
        compiler_params=params(),
        name="weight_spread",
    )(shares)


def exchange(array):
    return lax.all_to_all(array, AXES, split_axis=0, concat_axis=0, tiled=True)


def per_device(fields_in, lon_operator, w_in, w_out, inverses, cotangent):
    lat_tiles = lax.axis_size("lat")
    lon_tiles = lax.axis_size("lon")
    devices = lat_tiles * lon_tiles
    field_dev, _, grid_lon, grid_lat = fields_in.shape
    all_fields, all_levels, columns = cotangent.shape[2:]
    neurons, values = w_in.shape
    tile_lon = grid_lon // lon_tiles

    leaving = forward(
        fields_in.reshape(field_dev, grid_lon, grid_lat), lon_operator, lat_tiles, lon_tiles, tile_lon
    )
    arrived = exchange(leaving.reshape((devices,) + leaving.shape[2:]))

    matrix = inverses.reshape(all_levels, all_levels, columns)
    w_half = 0.5 * w_in
    grad_mixed = grad_mixed_of(matrix, cotangent.reshape(values, columns))

    going, cols = network(arrived, grad_mixed, w_half, w_out, lat_tiles)
    returned = exchange(going)

    diffused = diffused_of(cols, w_half, w_out, matrix, all_fields)

    shares = exchange(weight_sum(returned, diffused))
    grad_fields = adjoint(
        returned.reshape((lat_tiles, lon_tiles) + returned.shape[1:]), lon_operator, field_dev, grid_lat
    )
    grad_in, grad_out = weight_spread(shares, neurons, values)
    return (
        diffused.reshape(1, 1, all_fields, all_levels, columns),
        grad_fields.reshape(field_dev, 1, grid_lon, grid_lat),
        grad_in,
        grad_out,
    )


def solution(mesh):
    in_specs = (
        P("lat", "lon", None, None),
        P(),
        P(),
        P(),
        P("lat", "lon", None, None, None),
        P("lat", "lon", None, None, None),
    )
    out_specs = (P("lat", "lon", None, None, None), P("lat", "lon", None, None), P(), P())
    return jax.shard_map(
        per_device, mesh=mesh, in_specs=in_specs, out_specs=out_specs, check_vma=False
    )
```

time: 129 us -> 127 us (0.984)
  local copies, waits for them, and re-layouts: 5.33 us -> 3.63 us
    pallas_call x5, Pallas kernels: 30.8 us -> 29 us  [the longest x1 12.2 us: network(): pl.pallas_call(functools.partial(network_kernel, tiles=tiles), in_specs=[...]
    unnamed x12 -> x8, local copies, waits for them, and re-layouts: 5.33 us -> 3.63 us
    pallas_call x1, Pallas kernels: 22.2 us -> 23.7 us  [diffused_of(): pl.pallas_call(diffused_kernel, grid=(columns // chunk,), in_specs=[pl.Bl...]
where the time goes in v1:
time: 127 us
  Pallas kernels  66.1 us (52%)
  waiting for transfers between devices  36.1 us (28%)
  starting transfers between devices  19.6 us (15%)
  local copies, waits for them, and re-layouts  3.63 us (3%)
    all_to_all x3, waiting for transfers between devices, exchange(): return lax.all_to_all(array, AXES, split_axis=0, concat_axis=0, tiled=True)  36.1 us
    pallas_call x1, Pallas kernels, diffused_of(): pl.pallas_call(diffused_kernel, grid=(columns // chunk,), in_specs=[pl.Bl...  23.7 us
    all_to_all x3, starting transfers between devices, exchange(): return lax.all_to_all(array, AXES, split_axis=0, concat_axis=0, tiled=True)  19.6 us
    pallas_call x1, Pallas kernels, grad_mixed_of(): pl.pallas_call(grad_mixed_kernel, grid=(columns // chunk,), in_specs=[pl....  13.4 us
    pallas_call x1, Pallas kernels, network(): pl.pallas_call(functools.partial(network_kernel, tiles=tiles), in_specs=[...  12.2 us
    pallas_call x1, Pallas kernels, adjoint(): pl.pallas_call(adjoint_kernel, in_specs=[pl.BlockSpec(memory_space=pltpu....  6.42 us
    pallas_call x1, Pallas kernels, forward(): pl.pallas_call(forward_kernel, in_specs=[pl.BlockSpec(memory_space=pltpu....  6.4 us
    unnamed x8, local copies, waits for them, and re-layouts  3.63 us
  transfers between devices with their start and end apart: 3, of which 3 were waited for; matrix products, arithmetic and copies ran while one was open for 1% of the time, Pallas kernels for 34%

profile of v1, /device:TPU:1, one launch (start us, length us, event | category | flops | bytes accessed | tf_op | source)
XLA Modules:
  0.0 126.9 jit_solution(15008866853141216302)
XLA Ops:
  0.6 6.4 %forward_dynamics.1 = bf16[4,32,4,16,128]{4,3,2,1,0:T(8,128)(2,1)} custom-call(bf16[2,1024,512]{2,1,0:T(8,128)(2,1)} %bitcast.16, bf16[1024,1024]{1,0:T(8,128)(2,1)} %op_hbm.3), custom_call_target="tpu_custom_call" | custom-call | flops 2147483648 | bytes 6291456 | tf_op jit(solution)/shard_map/forward_dynamics/pallas_call | solution.py:97
  7.0 11.5 %all-to-all-start = ((bf16[128,4,16,128]{3,2,1,0:T(8,128)(2,1)}), bf16[128,4,16,128]{3,2,1,0:T(8,128)(2,1)S(1)}, u32[]{:S(2)}, u32[]{:S(2)}) async-start(bf16[128,4,16,128]{3,2,1,0:T(8,128)(2,1)} %bitcast.14), calls=%async_computation | async-start | bytes 4194304 | tf_op jit(solution)/shard_map/all_to_all | solution.py:501
  18.5 0.0 copy-start.3
  18.6 13.4 %grad_mixed.1.gm_hbm = bf16[256,4096]{1,0:T(8,128)(2,1)} custom-call(bf16[32,32,4096]{2,1,0:T(8,128)(2,1)} %bitcast.9, bf16[256,4096]{1,0:T(8,128)(2,1)} %bitcast.15), custom_call_target="tpu_custom_call" | custom-call | flops 67108864 | bytes 16777216 | tf_op jit(solution)/shard_map/grad_mixed/pallas_call | solution.py:140
  32.0 0.0 copy-done.3
  32.0 0.7 broadcast_multiply_fusion.w_half_hbm.w_half_ref
  32.7 16.3 %all-to-all-done.arrived_hbm = bf16[128,4,16,128]{3,2,1,0:T(8,128)(2,1)S(1)} async-done(((bf16[128,4,16,128]{3,2,1,0:T(8,128)(2,1)}), bf16[128,4,16,128]{3,2,1,0:T(8,128)(2,1)S(1)}, u32[]{:S(2)}, u32[]{:S(2)}) %all-to-all-start) | async-done | bytes 2097184 | tf_op jit(solution)/shard_map/all_to_all | solution.py:501
  49.0 0.0 copy-start.1
  49.0 1.3 %copy-done.1 = bf16[128,4,16,128]{3,2,1,0:T(8,128)(2,1)} copy-done((bf16[128,4,16,128]{3,2,1,0:T(8,128)(2,1)}, bf16[128,4,16,128]{3,2,1,0:T(8,128)(2,1)S(1)}, u32[]{:S(2)}) %copy-start.1) | copy-done | bytes 2097176
  50.3 12.2 %column_network.1 = (bf16[128,5,16,128]{3,2,1,0:T(8,128)(2,1)}, bf16[256,4096]{1,0:T(8,128)(2,1)}) custom-call(bf16[128,4,16,128]{3,2,1,0:T(8,128)(2,1)} %copy-done.1, bf16[256,4096]{1,0:T(8,128)(2,1)} %grad_mixed.1.gm_hbm, bf16[512,256]{1,0:T(8,128)(2,1)} %broadcast_multiply_fusion.w_half_hbm.w_half_ref, bf16[256,512]{1,0:T(8,128)(2,1)} %w_out_ref.1), custom_call_target="tpu_custom_call" | custom-call | flops 4294967296 | bytes 14680064 | tf_op jit(solution)/shard_map/column_network/pallas_call | solution.py:261
  62.5 4.0 %all-to-all-start.1 = ((bf16[128,5,16,128]{3,2,1,0:T(8,128)(2,1)}), bf16[128,5,16,128]{3,2,1,0:T(8,128)(2,1)S(1)}, u32[]{:S(2)}, u32[]{:S(2)}) async-start(bf16[128,5,16,128]{3,2,1,0:T(8,128)(2,1)} %get-tuple-element.9), calls=%async_computation.1 | async-start | bytes 5242880 | tf_op jit(solution)/shard_map/all_to_all | solution.py:501
  66.5 23.7 %diffused.1._ = f32[8,32,4096]{2,1,0:T(8,128)} custom-call(bf16[256,4096]{1,0:T(8,128)(2,1)} %get-tuple-element.8.cols_ref, bf16[512,256]{1,0:T(8,128)(2,1)} %broadcast_multiply_fusion.w_half_hbm.w_half_ref, bf16[256,512]{1,0:T(8,128)(2,1)} %w_out_ref.1, bf16[32,32,4096]{2,1,0:T(8,128)(2,1)} %bitcast.10), custom_call_target="tpu_custom_call" | custom-call | flops 2214592512 | bytes 16777216 | tf_op jit(solution)/shard_map/diffused/pallas_call | solution.py:319
  90.2 12.4 %all-to-all-done.1.returned_hbm = bf16[128,5,16,128]{3,2,1,0:T(8,128)(2,1)S(1)} async-done(((bf16[128,5,16,128]{3,2,1,0:T(8,128)(2,1)}), bf16[128,5,16,128]{3,2,1,0:T(8,128)(2,1)S(1)}, u32[]{:S(2)}, u32[]{:S(2)}) %all-to-all-start.1) | async-done | bytes 2621472 | tf_op jit(solution)/shard_map/all_to_all | solution.py:501
  102.6 0.0 copy-start
  102.6 1.5 %copy-done = bf16[128,5,16,128]{3,2,1,0:T(8,128)(2,1)} copy-done((bf16[128,5,16,128]{3,2,1,0:T(8,128)(2,1)}, bf16[128,5,16,128]{3,2,1,0:T(8,128)(2,1)S(1)}, u32[]{:S(2)}) %copy-start) | copy-done | bytes 2621464
  104.1 2.0 %weight_sum.1 = bf16[128,16,128]{2,1,0:T(8,128)(2,1)} custom-call(bf16[128,5,16,128]{3,2,1,0:T(8,128)(2,1)} %copy-done, f32[8,32,4096]{2,1,0:T(8,128)} %diffused.1._), custom_call_target="tpu_custom_call" | custom-call | flops 262144 | bytes 1048576 | tf_op jit(solution)/shard_map/weight_sum/pallas_call | solution.py:435
  106.1 4.1 %all-to-all-start.2 = ((bf16[128,16,128]{2,1,0:T(8,128)(2,1)}), bf16[128,16,128]{2,1,0:T(8,128)(2,1)S(1)}, u32[]{:S(2)}, u32[]{:S(2)}) async-start(bf16[128,16,128]{2,1,0:T(8,128)(2,1)} %weight_sum.1), calls=%async_computation.2 | async-start | bytes 1048576 | tf_op jit(solution)/shard_map/all_to_all | solution.py:501
  110.3 6.4 %adjoint_dynamics.1 = f32[2,1024,512]{2,1,0:T(8,128)} custom-call(bf16[4,32,5,16,128]{4,3,2,1,0:T(8,128)(2,1)} %bitcast.11, bf16[1024,1024]{1,0:T(8,128)(2,1)} %op_hbm.3), custom_call_target="tpu_custom_call" | custom-call | flops 2147483648 | bytes 8388608 | tf_op jit(solution)/shard_map/adjoint_dynamics/pallas_call | solution.py:390
  116.7 7.4 %all-to-all-done.2.shares_hbm = bf16[128,16,128]{2,1,0:T(8,128)(2,1)S(1)} async-done(((bf16[128,16,128]{2,1,0:T(8,128)(2,1)}), bf16[128,16,128]{2,1,0:T(8,128)(2,1)S(1)}, u32[]{:S(2)}, u32[]{:S(2)}) %all-to-all-start.2) | async-done | bytes 524320 | tf_op jit(solution)/shard_map/all_to_all | solution.py:501
  124.1 0.0 copy-start.2
  124.1 0.8 copy-done.2
  124.9 2.0 %weight_spread.1 = (f32[512,256]{1,0:T(8,128)}, f32[256,512]{1,0:T(8,128)}) custom-call(bf16[128,16,128]{2,1,0:T(8,128)(2,1)} %copy-done.2), custom_call_target="tpu_custom_call" | custom-call | tf_op jit(solution)/shard_map/weight_spread/pallas_call | solution.py:487
Async XLA Ops:
  7.0 42.0 %all-to-all-start = ((bf16[128,4,16,128]{3,2,1,0:T(8,128)(2,1)}), bf16[128,4,16,128]{3,2,1,0:T(8,128)(2,1)S(1)}, u32[]{:S(2)}, u32[]{:S(2)}) async-start(bf16[128,4,16,128]{3,2,1,0:T(8,128)(2,1)} %bitcast.14), calls=%async_computation | async-start | bytes 4194304 | tf_op jit(solution)/shard_map/all_to_all | solution.py:501
  18.5 13.4 %copy-start.3 = (bf16[512,256]{1,0:T(8,128)(2,1)S(1)}, bf16[512,256]{1,0:T(8,128)(2,1)}, u32[]{:S(2)}) copy-start(bf16[512,256]{1,0:T(8,128)(2,1)} %param.8) | copy-start | bytes 786436
  49.0 1.3 %copy-start.1 = (bf16[128,4,16,128]{3,2,1,0:T(8,128)(2,1)}, bf16[128,4,16,128]{3,2,1,0:T(8,128)(2,1)S(1)}, u32[]{:S(2)}) copy-start(bf16[128,4,16,128]{3,2,1,0:T(8,128)(2,1)S(1)} %all-to-all-done.arrived_hbm) | copy-start | bytes 6291460
  62.5 40.1 %all-to-all-start.1 = ((bf16[128,5,16,128]{3,2,1,0:T(8,128)(2,1)}), bf16[128,5,16,128]{3,2,1,0:T(8,128)(2,1)S(1)}, u32[]{:S(2)}, u32[]{:S(2)}) async-start(bf16[128,5,16,128]{3,2,1,0:T(8,128)(2,1)} %get-tuple-element.9), calls=%async_computation.1 | async-start | bytes 5242880 | tf_op jit(solution)/shard_map/all_to_all | solution.py:501
  102.6 1.5 %copy-start = (bf16[128,5,16,128]{3,2,1,0:T(8,128)(2,1)}, bf16[128,5,16,128]{3,2,1,0:T(8,128)(2,1)S(1)}, u32[]{:S(2)}) copy-start(bf16[128,5,16,128]{3,2,1,0:T(8,128)(2,1)S(1)} %all-to-all-done.1.returned_hbm) | copy-start | bytes 7864324
  106.1 17.9 %all-to-all-start.2 = ((bf16[128,16,128]{2,1,0:T(8,128)(2,1)}), bf16[128,16,128]{2,1,0:T(8,128)(2,1)S(1)}, u32[]{:S(2)}, u32[]{:S(2)}) async-start(bf16[128,16,128]{2,1,0:T(8,128)(2,1)} %weight_sum.1), calls=%async_computation.2 | async-start | bytes 1048576 | tf_op jit(solution)/shard_map/all_to_all | solution.py:501
  124.1 0.8 copy-start.2

commit v2 on v1

--- a/solution.py
+++ b/solution.py
@@ -13,11 +13,18 @@
 F32 = jnp.float32
 LANES = 128
 QROWS = 8
-VMEM_LIMIT = 60 * 1024 * 1024
-
-
-def params():
-    return pltpu.CompilerParams(vmem_limit_bytes=VMEM_LIMIT)
+
+
+def params(mebibytes=60):
+    return pltpu.CompilerParams(vmem_limit_bytes=mebibytes * 1024 * 1024)
+
+
+def in_vmem(x):
+    return pltpu.with_memory_space_constraint(x, pltpu.VMEM)
+
+
+def in_hbm(x):
+    return pltpu.with_memory_space_constraint(x, pltpu.HBM)
 
 
 def cost(flops, nbytes, trans=0):
@@ -98,7 +105,7 @@
         forward_kernel,
         in_specs=[pl.BlockSpec(memory_space=pltpu.HBM)] * 2,
         out_specs=pl.BlockSpec(memory_space=pltpu.HBM),
-        out_shape=jax.ShapeDtypeStruct(out_shape, BF),
+        out_shape=pltpu.HBM(out_shape, BF),
         scratch_shapes=[
             pltpu.VMEM(fields_in.shape, BF),
             pltpu.VMEM((blocks, grid_lon, block), BF),
@@ -110,7 +117,7 @@
         compiler_params=params(),
         cost_estimate=cost(2 * fields * grid_lon * grid_lon * grid_lat, 6 << 20),
         name="forward_dynamics",
-    )(fields_in, operator)
+    )(in_hbm(fields_in), in_hbm(operator))
 
 
 def grad_mixed_kernel(inv_ref, cot_ref, out_ref, wide):
@@ -145,37 +152,26 @@
             pl.BlockSpec((values, chunk), lambda i: (0, i)),
         ],
         out_specs=pl.BlockSpec((values, chunk), lambda i: (0, i)),
-        out_shape=jax.ShapeDtypeStruct((values, columns), BF),
+        out_shape=pltpu.HBM((values, columns), BF),
         scratch_shapes=[pltpu.VMEM((values, chunk), F32)],
-        compiler_params=params(),
+        compiler_params=params(40),
         cost_estimate=cost(2 * values * levels * columns, 16 << 20),
         name="grad_mixed",
-    )(matrix, incoming)
+    )(in_hbm(matrix), in_hbm(incoming))
 
 
 def network_kernel(
-    arrived_hbm, gm_hbm, w_half_hbm, w_out_hbm,
+    arrived, gm_hbm, w_half, w_out,
     leaving_hbm, cols_hbm,
-    arrived, gm, w_half, w_out, leaving, cols, act, grad_pre, wide_in, wide_out, acc_in, acc_out,
-    in_sem, w_sem, out_sem, *, tiles,
+    gm, leaving, cols, act, grad_pre, wide_in, wide_out, acc_in, acc_out, gm_sem, out_sem, *, tiles,
 ):
-    sources, steps, rows, _ = arrived_hbm.shape
+    sources, steps, rows, _ = arrived.shape
     fields = rows // QROWS
     group = sources // tiles
     chunk = QROWS * LANES
 
     def fetch(i):
-        lanes = pl.ds(i * chunk, chunk)
-        return (
-            pltpu.make_async_copy(arrived_hbm.at[:, i], arrived.at[i], in_sem.at[0, i]),
-            pltpu.make_async_copy(gm_hbm.at[:, lanes], gm.at[i], in_sem.at[1, i]),
-        )
-
-    def fetch_weights():
-        return [
-            pltpu.make_async_copy(w_half_hbm, w_half, w_sem.at[0]),
-            pltpu.make_async_copy(w_out_hbm, w_out, w_sem.at[1]),
-        ]
+        return pltpu.make_async_copy(gm_hbm.at[:, pl.ds(i * chunk, chunk)], gm.at[i], gm_sem.at[i])
 
     def store_leaving(i):
         return pltpu.make_async_copy(leaving.at[i], leaving_hbm.at[:, i], out_sem.at[0, i])
@@ -185,24 +181,12 @@
             cols.at[i], cols_hbm.at[:, pl.ds(i * chunk, chunk)], out_sem.at[1, i]
         )
 
-    weights = fetch_weights()
-    first = fetch(0)
-    first[0].start()
-    weights[0].start()
-    first[1].start()
-    weights[1].start()
-    for i in range(1, steps):
-        for copy in fetch(i):
-            copy.start()
+    for i in range(steps):
+        fetch(i).start()
     acc_in[...] = jnp.zeros_like(acc_in)
     acc_out[...] = jnp.zeros_like(acc_out)
-    for copy in weights:
-        copy.wait()
-
     def step(i, carry):
-        for copy in fetch(i):
-            copy.wait()
-        wide_in[...] = arrived[i].astype(F32).reshape(sources * rows, LANES)
+        wide_in[...] = arrived[:, i].astype(F32).reshape(sources * rows, LANES)
         for q in range(QROWS):
             by_field = [
                 wide_in[pl.ds(f * QROWS + q, sources, stride=rows), :] for f in range(fields)
@@ -211,6 +195,7 @@
                 by_field[f][a * group : (a + 1) * group] for a in range(tiles) for f in range(fields)
             ]
             cols[i, :, q * LANES : (q + 1) * LANES] = jnp.concatenate(parts, axis=0).astype(BF)
+        fetch(i).wait()
         half = dot(w_half[...], cols[i])
         turn = jnp.tanh(half)
         value = half + half * turn
@@ -260,17 +245,19 @@
     chunk = columns // steps
     return pl.pallas_call(
         functools.partial(network_kernel, tiles=tiles),
-        in_specs=[pl.BlockSpec(memory_space=pltpu.HBM)] * 4,
+        in_specs=[
+            pl.BlockSpec(memory_space=pltpu.VMEM),
+            pl.BlockSpec(memory_space=pltpu.HBM),
+            pl.BlockSpec(memory_space=pltpu.VMEM),
+            pl.BlockSpec(memory_space=pltpu.VMEM),
+        ],
         out_specs=[pl.BlockSpec(memory_space=pltpu.HBM)] * 2,
         out_shape=[
-            jax.ShapeDtypeStruct((sources, steps + 1, rows, LANES), BF),
-            jax.ShapeDtypeStruct((values, columns), BF),
+            pltpu.HBM((sources, steps + 1, rows, LANES), BF),
+            pltpu.HBM((values, columns), BF),
         ],
         scratch_shapes=[
-            pltpu.VMEM((steps, sources, rows, LANES), BF),
             pltpu.VMEM((steps, values, chunk), BF),
-            pltpu.VMEM((neurons, values), BF),
-            pltpu.VMEM((values, neurons), BF),
             pltpu.VMEM((steps + 1, sources, rows, LANES), BF),
             pltpu.VMEM((steps, values, chunk), BF),
             pltpu.VMEM((neurons, chunk), BF),
@@ -279,14 +266,13 @@
             pltpu.VMEM((sources * rows, LANES), F32),
             pltpu.VMEM((neurons, values), F32),
             pltpu.VMEM((neurons, values), F32),
-            pltpu.SemaphoreType.DMA((2, steps)),
-            pltpu.SemaphoreType.DMA((2,)),
+            pltpu.SemaphoreType.DMA((steps,)),
             pltpu.SemaphoreType.DMA((2, steps + 1)),
         ],
-        compiler_params=params(),
+        compiler_params=params(40),
         cost_estimate=cost(8 * neurons * values * columns, 14 << 20, neurons * columns),
         name="column_network",
-    )(arrived, grad_mixed, w_half, w_out)
+    )(in_vmem(arrived), in_hbm(grad_mixed), in_vmem(w_half), in_vmem(w_out))
 
 
 def diffused_kernel(cols_ref, w_half_ref, w_out_ref, inv_ref, out_ref, mixed, flat):
@@ -334,18 +320,16 @@
         compiler_params=params(),
         cost_estimate=cost(2 * values * (levels + 2 * neurons) * columns, 16 << 20),
         name="diffused",
-    )(cols, w_half, w_out, matrix)
-
-
-def adjoint_kernel(back_hbm, op_hbm, out_hbm, back, op_ref, grid_ref, out_ref, back_sem, op_sem, out_sem):
+    )(in_hbm(cols), w_half, w_out, in_hbm(matrix))
+
+
+def adjoint_kernel(back, op_hbm, out_hbm, op_ref, grid_ref, out_ref, op_sem, out_sem):
     fields = out_ref.shape[0]
-    tiles, lon_tiles, chunks, rows, _ = back.shape
+    tiles, lon_tiles = back.shape[:2]
     grid_lon = grid_ref.shape[1]
+    chunks = grid_lon // (lon_tiles * QROWS)
     block = 256
     blocks = grid_lon // block
-
-    def fetch_back(a):
-        return pltpu.make_async_copy(back_hbm.at[a, :, pl.ds(0, chunks)], back.at[a], back_sem.at[a])
 
     def fetch_op(i):
         part = pl.ds(i * block, block)
@@ -355,13 +339,10 @@
         part = pl.ds(i * block, block)
         return pltpu.make_async_copy(out_ref.at[f, part], out_hbm.at[f, part], out_sem.at[f, i])
 
-    for a in range(tiles):
-        fetch_back(a).start()
     for i in range(blocks):
         fetch_op(i).start()
     for a in range(tiles):
-        fetch_back(a).wait()
-        wide = back[a].astype(F32).reshape(lon_tiles * chunks, fields, QROWS, LANES)
+        wide = back[a, :, :chunks].astype(F32).reshape(lon_tiles * chunks, fields, QROWS, LANES)
         for f in range(fields):
             grid_ref[f, :, a * LANES : (a + 1) * LANES] = (
                 wide[:, f].reshape(grid_lon, LANES).astype(BF)
@@ -383,46 +364,29 @@
 
 
 def adjoint(returned, operator, fields, grid_lat):
-    tiles, lon_tiles, _, rows, _ = returned.shape
     grid_lon = operator.shape[0]
-    chunks = grid_lon // (lon_tiles * QROWS)
     blocks = grid_lon // 256
     return pl.pallas_call(
         adjoint_kernel,
-        in_specs=[pl.BlockSpec(memory_space=pltpu.HBM)] * 2,
+        in_specs=[pl.BlockSpec(memory_space=pltpu.VMEM), pl.BlockSpec(memory_space=pltpu.HBM)],
         out_specs=pl.BlockSpec(memory_space=pltpu.HBM),
         out_shape=jax.ShapeDtypeStruct((fields, grid_lon, grid_lat), F32),
         scratch_shapes=[
-            pltpu.VMEM((tiles, lon_tiles, chunks, rows, LANES), BF),
             pltpu.VMEM(operator.shape, BF),
             pltpu.VMEM((fields, grid_lon, grid_lat), BF),
             pltpu.VMEM((fields, grid_lon, grid_lat), F32),
-            pltpu.SemaphoreType.DMA((tiles,)),
             pltpu.SemaphoreType.DMA((blocks,)),
             pltpu.SemaphoreType.DMA((fields, blocks)),
         ],
-        compiler_params=params(),
+        compiler_params=params(48),
         cost_estimate=cost(2 * fields * grid_lon * grid_lon * grid_lat, 8 << 20),
         name="adjoint_dynamics",
-    )(returned, operator)
-
-
-def weight_sum_kernel(returned_hbm, _, out_hbm, parts, out_ref, in_sem, out_sem):
-    pieces = in_sem.shape[0]
-    each = parts.shape[0] // pieces
-    last = returned_hbm.shape[1] - 1
-
-    def fetch(k):
-        part = pl.ds(k * each, each)
-        return pltpu.make_async_copy(returned_hbm.at[part, last], parts.at[part], in_sem.at[k])
-
-    for k in range(pieces):
-        fetch(k).start()
-    total = None
-    for k in range(pieces):
-        fetch(k).wait()
-        piece = jnp.sum(parts[k * each : (k + 1) * each].astype(F32), axis=0, keepdims=True)
-        total = piece if total is None else total + piece
+    )(in_vmem(returned), in_hbm(operator))
+
+
+def weight_sum_kernel(returned, _, out_hbm, out_ref, out_sem):
+    last = returned.shape[1] - 1
+    total = jnp.sum(returned[:, last].astype(F32), axis=0, keepdims=True)
     out_ref[...] = jnp.broadcast_to(total.astype(BF), out_ref.shape)
     store = pltpu.make_async_copy(out_ref, out_hbm, out_sem)
     store.start()
@@ -434,32 +398,23 @@
     shape = (sources, rows, LANES)
     return pl.pallas_call(
         weight_sum_kernel,
-        in_specs=[pl.BlockSpec(memory_space=pltpu.HBM)] * 2,
+        in_specs=[pl.BlockSpec(memory_space=pltpu.VMEM), pl.BlockSpec(memory_space=pltpu.HBM)],
         out_specs=pl.BlockSpec(memory_space=pltpu.HBM),
-        out_shape=jax.ShapeDtypeStruct(shape, BF),
-        scratch_shapes=[
-            pltpu.VMEM(shape, BF),
-            pltpu.VMEM(shape, BF),
-            pltpu.SemaphoreType.DMA((4,)),
-            pltpu.SemaphoreType.DMA,
-        ],
-        compiler_params=params(),
+        out_shape=pltpu.HBM(shape, BF),
+        scratch_shapes=[pltpu.VMEM(shape, BF), pltpu.SemaphoreType.DMA],
+        compiler_params=params(48),
         cost_estimate=cost(sources * rows * LANES, 1 << 20),
         name="weight_sum",
-    )(returned, after)
-
-
-def weight_spread_kernel(shares_hbm, in_hbm, out_hbm, shares, in_ref, out_ref, in_sem, out_sem):
+    )(in_vmem(returned), in_hbm(after))
+
+
+def weight_spread_kernel(shares, in_hbm, out_hbm, in_ref, out_ref, out_sem):
     rows = shares.shape[1]
     height, breadth = in_ref.shape
     count = height // rows
     each = breadth // LANES
     jobs = 2 * each
 
-    def fetch(k):
-        part = pl.ds(k * count, count)
-        return pltpu.make_async_copy(shares_hbm.at[part], shares.at[part], in_sem.at[k])
-
     def store(k):
         part = pl.ds((k % each) * LANES, LANES)
         if k < each:
@@ -467,9 +422,6 @@
         return pltpu.make_async_copy(out_ref.at[part], out_hbm.at[part], out_sem.at[k])
 
     for k in range(jobs):
-        fetch(k).start()
-    for k in range(jobs):
-        fetch(k).wait()
         wide = shares[k * count : (k + 1) * count].astype(F32).reshape(height, LANES)
         part = slice((k % each) * LANES, (k % each + 1) * LANES)
         if k < each:
@@ -486,15 +438,14 @@
     jobs = 2 * (values // LANES)
     return pl.pallas_call(
         weight_spread_kernel,
-        in_specs=[pl.BlockSpec(memory_space=pltpu.HBM)],
+        in_specs=[pl.BlockSpec(memory_space=pltpu.VMEM)],
         out_specs=[pl.BlockSpec(memory_space=pltpu.HBM)] * 2,
         out_shape=[jax.ShapeDtypeStruct(shape, F32) for shape in shapes],
-        scratch_shapes=[pltpu.VMEM(shares.shape, BF)]
-        + [pltpu.VMEM(shape, F32) for shape in shapes]
-        + [pltpu.SemaphoreType.DMA((jobs,))] * 2,
-        compiler_params=params(),
+        scratch_shapes=[pltpu.VMEM(shape, F32) for shape in shapes]
+        + [pltpu.SemaphoreType.DMA((jobs,))],
+        compiler_params=params(48),
         name="weight_spread",
-    )(shares)
+    )(in_vmem(shares))
 
 
 def exchange(array):

time: 127 us -> 120 us (0.945)
  Pallas kernels: 66.1 us -> 61.8 us
  local copies, waits for them, and re-layouts: 3.63 us -> 0.02 us
  waiting for transfers between devices: 36.1 us -> 37.9 us
    unnamed x8 -> x6, local copies, waits for them, and re-layouts: 3.63 us -> 0.02 us
    all_to_all x3, waiting for transfers between devices: 36.1 us -> 37.9 us  [exchange(): return lax.all_to_all(array, AXES, split_axis=0, concat_axis=0, tiled=True)]
  transfers between devices with their start and end apart: 3 -> 3, of which waited for: 3 -> 3; matrix products, arithmetic and copies ran while one was open for 1% -> 0% of each run, Pallas kernels for 34% -> 35%
where the time goes in v2:
time: 120 us
  Pallas kernels  61.8 us (52%)
  waiting for transfers between devices  37.9 us (32%)
  starting transfers between devices  19.6 us (16%)
    all_to_all x3, waiting for transfers between devices, exchange(): return lax.all_to_all(array, AXES, split_axis=0, concat_axis=0, tiled=True)  37.9 us
    pallas_call x1, Pallas kernels, diffused_of(): pl.pallas_call(diffused_kernel, grid=(columns // chunk,), in_specs=[pl.Bl...  23.7 us
    all_to_all x3, starting transfers between devices, exchange(): return lax.all_to_all(array, AXES, split_axis=0, concat_axis=0, tiled=True)  19.6 us
    pallas_call x1, Pallas kernels, grad_mixed_of(): pl.pallas_call(grad_mixed_kernel, grid=(columns // chunk,), in_specs=[pl....  13.4 us
    pallas_call x1, Pallas kernels, network(): pl.pallas_call(functools.partial(network_kernel, tiles=tiles), in_specs=[...  10.9 us
    pallas_call x1, Pallas kernels, forward(): pl.pallas_call(forward_kernel, in_specs=[pl.BlockSpec(memory_space=pltpu....  6.39 us
    pallas_call x1, Pallas kernels, adjoint(): pl.pallas_call(adjoint_kernel, in_specs=[pl.BlockSpec(memory_space=pltpu....  5.35 us
  transfers between devices with their start and end apart: 3, of which 3 were waited for; matrix products, arithmetic and copies ran while one was open for 0% of the time, Pallas kernels for 35%

profile of v2, /device:TPU:1, one launch (start us, length us, event | category | flops | bytes accessed | tf_op | source)
XLA Modules:
  0.0 120.0 jit_solution(8643268630529894810)
XLA Ops:
  0.6 6.4 %forward_dynamics.1 = bf16[4,32,4,16,128]{4,3,2,1,0:T(8,128)(2,1)} custom-call(bf16[2,1024,512]{2,1,0:T(8,128)(2,1)} %bitcast.16, bf16[1024,1024]{1,0:T(8,128)(2,1)} %op_hbm.3), custom_call_target="tpu_custom_call" | custom-call | flops 2147483648 | bytes 6291456 | tf_op jit(solution)/shard_map/forward_dynamics/pallas_call | solution.py:104
  7.0 11.5 %all-to-all-start = ((bf16[128,4,16,128]{3,2,1,0:T(8,128)(2,1)}), bf16[128,4,16,128]{3,2,1,0:T(8,128)(2,1)S(1)}, u32[]{:S(2)}, u32[]{:S(2)}) async-start(bf16[128,4,16,128]{3,2,1,0:T(8,128)(2,1)} %bitcast.14), calls=%async_computation | async-start | bytes 4194304 | tf_op jit(solution)/shard_map/all_to_all | solution.py:452
  18.5 0.0 copy-start.2
  18.6 0.0 copy-start.1
  18.6 13.4 %grad_mixed.1.gm_hbm = bf16[256,4096]{1,0:T(8,128)(2,1)} custom-call(bf16[32,32,4096]{2,1,0:T(8,128)(2,1)} %bitcast.10, bf16[256,4096]{1,0:T(8,128)(2,1)} %bitcast.15), custom_call_target="tpu_custom_call" | custom-call | flops 67108864 | bytes 16777216 | tf_op jit(solution)/shard_map/grad_mixed/pallas_call | solution.py:147
  32.0 0.0 copy-done.2
  32.0 0.0 copy-start
  32.0 17.0 %all-to-all-done.arrived = bf16[128,4,16,128]{3,2,1,0:T(8,128)(2,1)S(1)} async-done(((bf16[128,4,16,128]{3,2,1,0:T(8,128)(2,1)}), bf16[128,4,16,128]{3,2,1,0:T(8,128)(2,1)S(1)}, u32[]{:S(2)}, u32[]{:S(2)}) %all-to-all-start) | async-done | bytes 2097184 | tf_op jit(solution)/shard_map/all_to_all | solution.py:452
  49.0 0.0 copy-done.1
  49.0 10.9 %column_network.1 = (bf16[128,5,16,128]{3,2,1,0:T(8,128)(2,1)}, bf16[256,4096]{1,0:T(8,128)(2,1)}) custom-call(bf16[128,4,16,128]{3,2,1,0:T(8,128)(2,1)S(1)} %all-to-all-done.arrived, bf16[256,4096]{1,0:T(8,128)(2,1)} %grad_mixed.1.gm_hbm, bf16[512,256]{1,0:T(8,128)(2,1)S(1)} %broadcast_multiply_fusion.w_half.w_half_ref, bf16[256,512]{1,0:T(8,128)(2,1)S(1)} %copy-done.1), custom_call_target="tpu_custom_call" | custom-call | flops 4294967296 | bytes 14680064 | tf_op jit(solution)/shard_map/column_network/pallas_call | solution.py:246
  59.9 0.0 copy-done
  60.0 4.0 %all-to-all-start.1 = ((bf16[128,5,16,128]{3,2,1,0:T(8,128)(2,1)}), bf16[128,5,16,128]{3,2,1,0:T(8,128)(2,1)S(1)}, u32[]{:S(2)}, u32[]{:S(2)}) async-start(bf16[128,5,16,128]{3,2,1,0:T(8,128)(2,1)} %get-tuple-element.9), calls=%async_computation.1 | async-start | bytes 5242880 | tf_op jit(solution)/shard_map/all_to_all | solution.py:452
  64.0 23.7 %diffused.1._ = f32[8,32,4096]{2,1,0:T(8,128)} custom-call(bf16[256,4096]{1,0:T(8,128)(2,1)} %get-tuple-element.8.cols_ref, bf16[512,256]{1,0:T(8,128)(2,1)} %copy-done, bf16[256,512]{1,0:T(8,128)(2,1)} %w_out_ref.1, bf16[32,32,4096]{2,1,0:T(8,128)(2,1)} %bitcast.11), custom_call_target="tpu_custom_call" | custom-call | flops 2214592512 | bytes 16777216 | tf_op jit(solution)/shard_map/diffused/pallas_call | solution.py:305
  87.7 12.4 %all-to-all-done.1.returned = bf16[128,5,16,128]{3,2,1,0:T(8,128)(2,1)S(1)} async-done(((bf16[128,5,16,128]{3,2,1,0:T(8,128)(2,1)}), bf16[128,5,16,128]{3,2,1,0:T(8,128)(2,1)S(1)}, u32[]{:S(2)}, u32[]{:S(2)}) %all-to-all-start.1) | async-done | bytes 2621472 | tf_op jit(solution)/shard_map/all_to_all | solution.py:452
  100.1 1.0 weight_sum.1
  101.0 4.1 %all-to-all-start.2 = ((bf16[128,16,128]{2,1,0:T(8,128)(2,1)}), bf16[128,16,128]{2,1,0:T(8,128)(2,1)S(1)}, u32[]{:S(2)}, u32[]{:S(2)}) async-start(bf16[128,16,128]{2,1,0:T(8,128)(2,1)} %weight_sum.1), calls=%async_computation.2 | async-start | bytes 1048576 | tf_op jit(solution)/shard_map/all_to_all | solution.py:452
  105.2 5.3 %adjoint_dynamics.1 = f32[2,1024,512]{2,1,0:T(8,128)} custom-call(bf16[4,32,5,16,128]{4,3,2,1,0:T(8,128)(2,1)S(1)} %bitcast.9, bf16[1024,1024]{1,0:T(8,128)(2,1)} %op_hbm.3), custom_call_target="tpu_custom_call" | custom-call | flops 2147483648 | bytes 8388608 | tf_op jit(solution)/shard_map/adjoint_dynamics/pallas_call | solution.py:369
  110.5 8.5 %all-to-all-done.2.shares = bf16[128,16,128]{2,1,0:T(8,128)(2,1)S(1)} async-done(((bf16[128,16,128]{2,1,0:T(8,128)(2,1)}), bf16[128,16,128]{2,1,0:T(8,128)(2,1)S(1)}, u32[]{:S(2)}, u32[]{:S(2)}) %all-to-all-start.2) | async-done | bytes 524320 | tf_op jit(solution)/shard_map/all_to_all | solution.py:452
  119.0 1.0 weight_spread.1
  (1 shorter events, 0.0 us)
Async XLA Ops:
  7.0 42.0 %all-to-all-start = ((bf16[128,4,16,128]{3,2,1,0:T(8,128)(2,1)}), bf16[128,4,16,128]{3,2,1,0:T(8,128)(2,1)S(1)}, u32[]{:S(2)}, u32[]{:S(2)}) async-start(bf16[128,4,16,128]{3,2,1,0:T(8,128)(2,1)} %bitcast.14), calls=%async_computation | async-start | bytes 4194304 | tf_op jit(solution)/shard_map/all_to_all | solution.py:452
  18.5 13.4 %copy-start.2 = (bf16[512,256]{1,0:T(8,128)(2,1)S(1)}, bf16[512,256]{1,0:T(8,128)(2,1)}, u32[]{:S(2)}) copy-start(bf16[512,256]{1,0:T(8,128)(2,1)} %param.8) | copy-start | bytes 786436
  18.6 30.5 %copy-start.1 = (bf16[256,512]{1,0:T(8,128)(2,1)S(1)}, bf16[256,512]{1,0:T(8,128)(2,1)}, u32[]{:S(2)}) copy-start(bf16[256,512]{1,0:T(8,128)(2,1)} %w_out_ref.1) | copy-start | bytes 786436
  32.0 27.9 %copy-start = (bf16[512,256]{1,0:T(8,128)(2,1)}, bf16[512,256]{1,0:T(8,128)(2,1)S(1)}, u32[]{:S(2)}) copy-start(bf16[512,256]{1,0:T(8,128)(2,1)S(1)} %broadcast_multiply_fusion.w_half.w_half_ref) | copy-start | bytes 786436
  60.0 40.1 %all-to-all-start.1 = ((bf16[128,5,16,128]{3,2,1,0:T(8,128)(2,1)}), bf16[128,5,16,128]{3,2,1,0:T(8,128)(2,1)S(1)}, u32[]{:S(2)}, u32[]{:S(2)}) async-start(bf16[128,5,16,128]{3,2,1,0:T(8,128)(2,1)} %get-tuple-element.9), calls=%async_computation.1 | async-start | bytes 5242880 | tf_op jit(solution)/shard_map/all_to_all | solution.py:452
  101.0 17.9 %all-to-all-start.2 = ((bf16[128,16,128]{2,1,0:T(8,128)(2,1)}), bf16[128,16,128]{2,1,0:T(8,128)(2,1)S(1)}, u32[]{:S(2)}, u32[]{:S(2)}) async-start(bf16[128,16,128]{2,1,0:T(8,128)(2,1)} %weight_sum.1), calls=%async_computation.2 | async-start | bytes 1048576 | tf_op jit(solution)/shard_map/all_to_all | solution.py:452

commit v3 on v2

--- a/solution.py
+++ b/solution.py
@@ -13,6 +13,7 @@
 F32 = jnp.float32
 LANES = 128
 QROWS = 8
+PAD = 8
 
 
 def params(mebibytes=60):
@@ -169,6 +170,7 @@
     fields = rows // QROWS
     group = sources // tiles
     chunk = QROWS * LANES
+    pitch = wide_in.shape[0] // (sources + 1)
 
     def fetch(i):
         return pltpu.make_async_copy(gm_hbm.at[:, pl.ds(i * chunk, chunk)], gm.at[i], gm_sem.at[i])
@@ -185,26 +187,28 @@
         fetch(i).start()
     acc_in[...] = jnp.zeros_like(acc_in)
     acc_out[...] = jnp.zeros_like(acc_out)
+
     def step(i, carry):
-        wide_in[...] = arrived[:, i].astype(F32).reshape(sources * rows, LANES)
+        for s in range(sources):
+            wide_in[s * pitch : s * pitch + rows, :] = arrived[s, i].astype(F32)
         for q in range(QROWS):
             by_field = [
-                wide_in[pl.ds(f * QROWS + q, sources, stride=rows), :] for f in range(fields)
+                wide_in[pl.ds(f * QROWS + q, sources, stride=pitch), :] for f in range(fields)
             ]
             parts = [
                 by_field[f][a * group : (a + 1) * group] for a in range(tiles) for f in range(fields)
             ]
             cols[i, :, q * LANES : (q + 1) * LANES] = jnp.concatenate(parts, axis=0).astype(BF)
-        fetch(i).wait()
         half = dot(w_half[...], cols[i])
         turn = jnp.tanh(half)
         value = half + half * turn
         act[...] = value.astype(BF)
+        fetch(i).wait()
         slope = 1.0 + (turn + value) - turn * value
         grad_pre[...] = (dot(w_out[...], gm[i], (0, 0)) * slope).astype(BF)
-        grad_cols = gm[i].astype(F32) + dot(w_half[...], grad_pre[...], (0, 0))
         acc_in[...] += dot(grad_pre[...], cols[i], (1, 1))
         acc_out[...] += dot(act[...], gm[i], (1, 1))
+        grad_cols = gm[i].astype(F32) + dot(w_half[...], grad_pre[...], (0, 0))
         for q in range(QROWS):
             piece = grad_cols[:, q * LANES : (q + 1) * LANES]
             for f in range(fields):
@@ -212,10 +216,11 @@
                     piece[(a * fields + f) * group : (a * fields + f + 1) * group]
                     for a in range(tiles)
                 ]
-                wide_out[pl.ds(f * QROWS + q, sources, stride=rows), :] = jnp.concatenate(
+                wide_out[pl.ds(f * QROWS + q, sources, stride=pitch), :] = jnp.concatenate(
                     parts, axis=0
                 )
-        leaving[i] = wide_out[...].reshape(sources, rows, LANES).astype(BF)
+        for s in range(sources):
+            leaving[i, s] = wide_out[s * pitch : s * pitch + rows, :].astype(BF)
         store_cols(i).start()
         store_leaving(i).start()
         return carry
@@ -262,8 +267,8 @@
             pltpu.VMEM((steps, values, chunk), BF),
             pltpu.VMEM((neurons, chunk), BF),
             pltpu.VMEM((neurons, chunk), BF),
-            pltpu.VMEM((sources * rows, LANES), F32),
-            pltpu.VMEM((sources * rows, LANES), F32),
+            pltpu.VMEM(((sources + 1) * (rows + PAD), LANES), F32),
+            pltpu.VMEM(((sources + 1) * (rows + PAD), LANES), F32),
             pltpu.VMEM((neurons, values), F32),
             pltpu.VMEM((neurons, values), F32),
             pltpu.SemaphoreType.DMA((steps,)),
@@ -284,7 +289,7 @@
 
     def tile(t, carry):
         lanes = pl.ds(pl.multiple_of(t * LANES, LANES), LANES)
-        flat[...] = inv_ref[:, :, lanes].astype(F32).reshape(levels * levels, LANES)
+        flat[: levels * levels] = inv_ref[:, :, lanes].astype(F32).reshape(levels * levels, LANES)
         acc = [None] * fields
         for m in range(levels):
             matrix = flat[pl.ds(m, levels, stride=levels), :]
@@ -315,7 +320,7 @@
         out_shape=jax.ShapeDtypeStruct((fields, levels, columns), F32),
         scratch_shapes=[
             pltpu.VMEM((values, chunk), F32),
-            pltpu.VMEM((levels * levels, LANES), F32),
+            pltpu.VMEM(((levels + 1) * levels, LANES), F32),
         ],
         compiler_params=params(),
         cost_estimate=cost(2 * values * (levels + 2 * neurons) * columns, 16 << 20),

time: 120 us -> 119 us (level)
  Pallas kernels: 61.8 us -> 60.5 us
    pallas_call x1, Pallas kernels: 10.9 us -> 9.59 us  [network(): pl.pallas_call(functools.partial(network_kernel, tiles=tiles), in_specs=[...]
  transfers between devices with their start and end apart: 3 -> 3, of which waited for: 3 -> 3; matrix products, arithmetic and copies ran while one was open for 0% -> 0% of each run, Pallas kernels for 35% -> 36%
where the time goes in v3:
time: 119 us
  Pallas kernels  60.5 us (51%)
  waiting for transfers between devices  37.9 us (32%)
  starting transfers between devices  19.6 us (16%)
    all_to_all x3, waiting for transfers between devices, exchange(): return lax.all_to_all(array, AXES, split_axis=0, concat_axis=0, tiled=True)  37.9 us
    pallas_call x1, Pallas kernels, diffused_of(): pl.pallas_call(diffused_kernel, grid=(columns // chunk,), in_specs=[pl.Bl...  23.7 us
    all_to_all x3, starting transfers between devices, exchange(): return lax.all_to_all(array, AXES, split_axis=0, concat_axis=0, tiled=True)  19.6 us
    pallas_call x1, Pallas kernels, grad_mixed_of(): pl.pallas_call(grad_mixed_kernel, grid=(columns // chunk,), in_specs=[pl....  13.4 us
    pallas_call x1, Pallas kernels, network(): pl.pallas_call(functools.partial(network_kernel, tiles=tiles), in_specs=[...  9.59 us
    pallas_call x1, Pallas kernels, forward(): pl.pallas_call(forward_kernel, in_specs=[pl.BlockSpec(memory_space=pltpu....  6.39 us
    pallas_call x1, Pallas kernels, adjoint(): pl.pallas_call(adjoint_kernel, in_specs=[pl.BlockSpec(memory_space=pltpu....  5.35 us
  transfers between devices with their start and end apart: 3, of which 3 were waited for; matrix products, arithmetic and copies ran while one was open for 0% of the time, Pallas kernels for 36%

profile of v3, /device:TPU:1, one launch (start us, length us, event | category | flops | bytes accessed | tf_op | source)
XLA Modules:
  0.0 118.7 jit_solution(3527638770443699800)
XLA Ops:
  0.6 6.4 %forward_dynamics.1 = bf16[4,32,4,16,128]{4,3,2,1,0:T(8,128)(2,1)} custom-call(bf16[2,1024,512]{2,1,0:T(8,128)(2,1)} %bitcast.16, bf16[1024,1024]{1,0:T(8,128)(2,1)} %op_hbm.3), custom_call_target="tpu_custom_call" | custom-call | flops 2147483648 | bytes 6291456 | tf_op jit(solution)/shard_map/forward_dynamics/pallas_call | solution.py:105
  7.0 11.5 %all-to-all-start = ((bf16[128,4,16,128]{3,2,1,0:T(8,128)(2,1)}), bf16[128,4,16,128]{3,2,1,0:T(8,128)(2,1)S(1)}, u32[]{:S(2)}, u32[]{:S(2)}) async-start(bf16[128,4,16,128]{3,2,1,0:T(8,128)(2,1)} %bitcast.14), calls=%async_computation | async-start | bytes 4194304 | tf_op jit(solution)/shard_map/all_to_all | solution.py:457
  18.5 0.0 copy-start.2
  18.6 0.0 copy-start.1
  18.6 13.4 %grad_mixed.1.gm_hbm = bf16[256,4096]{1,0:T(8,128)(2,1)} custom-call(bf16[32,32,4096]{2,1,0:T(8,128)(2,1)} %bitcast.10, bf16[256,4096]{1,0:T(8,128)(2,1)} %bitcast.15), custom_call_target="tpu_custom_call" | custom-call | flops 67108864 | bytes 16777216 | tf_op jit(solution)/shard_map/grad_mixed/pallas_call | solution.py:148
  32.0 0.0 copy-done.2
  32.0 0.0 copy-start
  32.0 17.0 %all-to-all-done.arrived = bf16[128,4,16,128]{3,2,1,0:T(8,128)(2,1)S(1)} async-done(((bf16[128,4,16,128]{3,2,1,0:T(8,128)(2,1)}), bf16[128,4,16,128]{3,2,1,0:T(8,128)(2,1)S(1)}, u32[]{:S(2)}, u32[]{:S(2)}) %all-to-all-start) | async-done | bytes 2097184 | tf_op jit(solution)/shard_map/all_to_all | solution.py:457
  49.0 0.0 copy-done.1
  49.0 9.6 %column_network.1 = (bf16[128,5,16,128]{3,2,1,0:T(8,128)(2,1)}, bf16[256,4096]{1,0:T(8,128)(2,1)}) custom-call(bf16[128,4,16,128]{3,2,1,0:T(8,128)(2,1)S(1)} %all-to-all-done.arrived, bf16[256,4096]{1,0:T(8,128)(2,1)} %grad_mixed.1.gm_hbm, bf16[512,256]{1,0:T(8,128)(2,1)S(1)} %broadcast_multiply_fusion.w_half.w_half_ref, bf16[256,512]{1,0:T(8,128)(2,1)S(1)} %copy-done.1), custom_call_target="tpu_custom_call" | custom-call | flops 4294967296 | bytes 14680064 | tf_op jit(solution)/shard_map/column_network/pallas_call | solution.py:251
  58.6 0.0 copy-done
  58.6 4.0 %all-to-all-start.1 = ((bf16[128,5,16,128]{3,2,1,0:T(8,128)(2,1)}), bf16[128,5,16,128]{3,2,1,0:T(8,128)(2,1)S(1)}, u32[]{:S(2)}, u32[]{:S(2)}) async-start(bf16[128,5,16,128]{3,2,1,0:T(8,128)(2,1)} %get-tuple-element.9), calls=%async_computation.1 | async-start | bytes 5242880 | tf_op jit(solution)/shard_map/all_to_all | solution.py:457
  62.6 23.7 %diffused.1._ = f32[8,32,4096]{2,1,0:T(8,128)} custom-call(bf16[256,4096]{1,0:T(8,128)(2,1)} %get-tuple-element.8.cols_ref, bf16[512,256]{1,0:T(8,128)(2,1)} %copy-done, bf16[256,512]{1,0:T(8,128)(2,1)} %w_out_ref.1, bf16[32,32,4096]{2,1,0:T(8,128)(2,1)} %bitcast.11), custom_call_target="tpu_custom_call" | custom-call | flops 2214592512 | bytes 16777216 | tf_op jit(solution)/shard_map/diffused/pallas_call | solution.py:310
  86.3 12.4 %all-to-all-done.1.returned = bf16[128,5,16,128]{3,2,1,0:T(8,128)(2,1)S(1)} async-done(((bf16[128,5,16,128]{3,2,1,0:T(8,128)(2,1)}), bf16[128,5,16,128]{3,2,1,0:T(8,128)(2,1)S(1)}, u32[]{:S(2)}, u32[]{:S(2)}) %all-to-all-start.1) | async-done | bytes 2621472 | tf_op jit(solution)/shard_map/all_to_all | solution.py:457
  98.7 1.0 weight_sum.1
  99.7 4.1 %all-to-all-start.2 = ((bf16[128,16,128]{2,1,0:T(8,128)(2,1)}), bf16[128,16,128]{2,1,0:T(8,128)(2,1)S(1)}, u32[]{:S(2)}, u32[]{:S(2)}) async-start(bf16[128,16,128]{2,1,0:T(8,128)(2,1)} %weight_sum.1), calls=%async_computation.2 | async-start | bytes 1048576 | tf_op jit(solution)/shard_map/all_to_all | solution.py:457
  103.8 5.3 %adjoint_dynamics.1 = f32[2,1024,512]{2,1,0:T(8,128)} custom-call(bf16[4,32,5,16,128]{4,3,2,1,0:T(8,128)(2,1)S(1)} %bitcast.9, bf16[1024,1024]{1,0:T(8,128)(2,1)} %op_hbm.3), custom_call_target="tpu_custom_call" | custom-call | flops 2147483648 | bytes 8388608 | tf_op jit(solution)/shard_map/adjoint_dynamics/pallas_call | solution.py:374
  109.2 8.5 %all-to-all-done.2.shares = bf16[128,16,128]{2,1,0:T(8,128)(2,1)S(1)} async-done(((bf16[128,16,128]{2,1,0:T(8,128)(2,1)}), bf16[128,16,128]{2,1,0:T(8,128)(2,1)S(1)}, u32[]{:S(2)}, u32[]{:S(2)}) %all-to-all-start.2) | async-done | bytes 524320 | tf_op jit(solution)/shard_map/all_to_all | solution.py:457
  117.7 1.0 weight_spread.1
  (1 shorter events, 0.0 us)
Async XLA Ops:
  7.0 42.0 %all-to-all-start = ((bf16[128,4,16,128]{3,2,1,0:T(8,128)(2,1)}), bf16[128,4,16,128]{3,2,1,0:T(8,128)(2,1)S(1)}, u32[]{:S(2)}, u32[]{:S(2)}) async-start(bf16[128,4,16,128]{3,2,1,0:T(8,128)(2,1)} %bitcast.14), calls=%async_computation | async-start | bytes 4194304 | tf_op jit(solution)/shard_map/all_to_all | solution.py:457
  18.5 13.4 %copy-start.2 = (bf16[512,256]{1,0:T(8,128)(2,1)S(1)}, bf16[512,256]{1,0:T(8,128)(2,1)}, u32[]{:S(2)}) copy-start(bf16[512,256]{1,0:T(8,128)(2,1)} %param.8) | copy-start | bytes 786436
  18.6 30.5 %copy-start.1 = (bf16[256,512]{1,0:T(8,128)(2,1)S(1)}, bf16[256,512]{1,0:T(8,128)(2,1)}, u32[]{:S(2)}) copy-start(bf16[256,512]{1,0:T(8,128)(2,1)} %w_out_ref.1) | copy-start | bytes 786436
  32.0 26.6 %copy-start = (bf16[512,256]{1,0:T(8,128)(2,1)}, bf16[512,256]{1,0:T(8,128)(2,1)S(1)}, u32[]{:S(2)}) copy-start(bf16[512,256]{1,0:T(8,128)(2,1)S(1)} %broadcast_multiply_fusion.w_half.w_half_ref) | copy-start | bytes 786436
  58.6 40.1 %all-to-all-start.1 = ((bf16[128,5,16,128]{3,2,1,0:T(8,128)(2,1)}), bf16[128,5,16,128]{3,2,1,0:T(8,128)(2,1)S(1)}, u32[]{:S(2)}, u32[]{:S(2)}) async-start(bf16[128,5,16,128]{3,2,1,0:T(8,128)(2,1)} %get-tuple-element.9), calls=%async_computation.1 | async-start | bytes 5242880 | tf_op jit(solution)/shard_map/all_to_all | solution.py:457
  99.7 17.9 %all-to-all-start.2 = ((bf16[128,16,128]{2,1,0:T(8,128)(2,1)}), bf16[128,16,128]{2,1,0:T(8,128)(2,1)S(1)}, u32[]{:S(2)}, u32[]{:S(2)}) async-start(bf16[128,16,128]{2,1,0:T(8,128)(2,1)} %weight_sum.1), calls=%async_computation.2 | async-start | bytes 1048576 | tf_op jit(solution)/shard_map/all_to_all | solution.py:457

commit v4 on v3

--- a/solution.py
+++ b/solution.py
@@ -36,6 +36,13 @@
     return lax.dot_general(a, b, (((dims[0],), (dims[1],)), ((), ())), preferred_element_type=F32)
 
 
+def stencil(size):
+    row = lax.broadcasted_iota(jnp.int32, (size, size), 0)
+    lane = lax.broadcasted_iota(jnp.int32, (size, size), 1)
+    apart = jnp.abs(row - lane)
+    return jnp.where(apart == 0, 1.0 / KAPPA - 2.0, jnp.where(apart == 1, 1.0, 0.0)).astype(BF)
+
+
 def spread(wide):
     size = wide.shape[1]
     lane = lax.broadcasted_iota(jnp.int32, wide.shape, 1)
@@ -44,7 +51,7 @@
     return (1.0 - 2.0 * KAPPA) * wide + KAPPA * (after + before)
 
 
-def forward_kernel(v_hbm, op_hbm, out_hbm, v_ref, op_ref, out_ref, v_sem, op_sem, out_sem):
+def forward_kernel(v_hbm, op_hbm, out_hbm, v_ref, op_ref, out_ref, near, side, v_sem, op_sem, out_sem):
     fields = v_ref.shape[0]
     blocks = op_ref.shape[0]
     block = op_ref.shape[2]
@@ -62,25 +69,26 @@
         part = pl.ds(i * per_block, per_block)
         return pltpu.make_async_copy(out_ref.at[:, part], out_hbm.at[:, part], out_sem.at[i])
 
-    fetch_op(0).start()
     for f in range(fields):
         fetch_v(f).start()
-    for i in range(1, blocks):
+    for i in range(blocks):
         fetch_op(i).start()
+    near[...] = stencil(near.shape[0])
+
+    def across(f, carry):
+        fetch_v(f).wait()
+        side[f] = KAPPA * dot(v_ref[f], near[...])
+        return carry
+
+    lax.fori_loop(0, fields, across, 0)
     def step(i, carry):
         fetch_op(i).wait()
-
-        @pl.when(i == 0)
-        def _():
-            for f in range(fields):
-                fetch_v(f).wait()
 
         rows_here = pl.ds(pl.multiple_of(i * block, block), block)
         done = []
         for f in range(fields):
             along = dot(op_ref[i], v_ref[f], (0, 0))
-            wide = v_ref[f, rows_here, :].astype(F32)
-            done.append(along + spread(wide))
+            done.append(along + side[f, rows_here, :])
         for a in range(tiles):
             parts = [
                 d[:, a * LANES : (a + 1) * LANES].reshape(per_block, chunks, 1, QROWS, LANES)
@@ -99,7 +107,7 @@
 def forward(fields_in, operator, lat_tiles, lon_tiles, tile_lon):
     fields, grid_lon, grid_lat = fields_in.shape
     chunks = tile_lon // QROWS
-    block = 256
+    block = 512
     blocks = grid_lon // block
     out_shape = (lat_tiles, lon_tiles, chunks, fields * QROWS, LANES)
     return pl.pallas_call(
@@ -111,6 +119,8 @@
             pltpu.VMEM(fields_in.shape, BF),
             pltpu.VMEM((blocks, grid_lon, block), BF),
             pltpu.VMEM(out_shape, BF),
+            pltpu.VMEM((grid_lat, grid_lat), BF),
+            pltpu.VMEM(fields_in.shape, F32),
             pltpu.SemaphoreType.DMA((fields,)),
             pltpu.SemaphoreType.DMA((blocks,)),
             pltpu.SemaphoreType.DMA((blocks,)),
@@ -391,11 +401,26 @@
 
 def weight_sum_kernel(returned, _, out_hbm, out_ref, out_sem):
     last = returned.shape[1] - 1
-    total = jnp.sum(returned[:, last].astype(F32), axis=0, keepdims=True)
-    out_ref[...] = jnp.broadcast_to(total.astype(BF), out_ref.shape)
-    store = pltpu.make_async_copy(out_ref, out_hbm, out_sem)
-    store.start()
-    store.wait()
+    sources = out_ref.shape[0]
+    lanes = 8
+    partial = [returned[k, last].astype(F32) for k in range(lanes)]
+    for k in range(lanes, sources):
+        partial[k % lanes] = partial[k % lanes] + returned[k, last].astype(F32)
+    while len(partial) > 1:
+        partial = [a + b for a, b in zip(partial[::2], partial[1::2])]
+    total = partial[0].astype(BF)
+    pieces = out_sem.shape[0]
+    each = sources // pieces
+
+    def store(k):
+        part = pl.ds(k * each, each)
+        return pltpu.make_async_copy(out_ref.at[part], out_hbm.at[part], out_sem.at[k])
+
+    for k in range(pieces):
+        out_ref[k * each : (k + 1) * each] = jnp.broadcast_to(total[None], (each,) + total.shape)
+        store(k).start()
+    for k in range(pieces):
+        store(k).wait()
 
 
 def weight_sum(returned, after):
@@ -406,7 +431,7 @@
         in_specs=[pl.BlockSpec(memory_space=pltpu.VMEM), pl.BlockSpec(memory_space=pltpu.HBM)],
         out_specs=pl.BlockSpec(memory_space=pltpu.HBM),
         out_shape=pltpu.HBM(shape, BF),
-        scratch_shapes=[pltpu.VMEM(shape, BF), pltpu.SemaphoreType.DMA],
+        scratch_shapes=[pltpu.VMEM(shape, BF), pltpu.SemaphoreType.DMA((1,))],
         compiler_params=params(48),
         cost_estimate=cost(sources * rows * LANES, 1 << 20),
         name="weight_sum",

time: 119 us -> 119 us (level)
  no operation moved by 1% of the time
where the time goes in v4:
time: 119 us; the launch traced here: 118 us
  Pallas kernels  60.2 us (51%)
  waiting for transfers between devices  37.9 us (32%)
  starting transfers between devices  19.6 us (16%)
    all_to_all x3, waiting for transfers between devices, exchange(): return lax.all_to_all(array, AXES, split_axis=0, concat_axis=0, tiled=True)  37.9 us
    pallas_call x1, Pallas kernels, diffused_of(): pl.pallas_call(diffused_kernel, grid=(columns // chunk,), in_specs=[pl.Bl...  23.7 us
    all_to_all x3, starting transfers between devices, exchange(): return lax.all_to_all(array, AXES, split_axis=0, concat_axis=0, tiled=True)  19.6 us
    pallas_call x1, Pallas kernels, grad_mixed_of(): pl.pallas_call(grad_mixed_kernel, grid=(columns // chunk,), in_specs=[pl....  13.4 us
    pallas_call x1, Pallas kernels, network(): pl.pallas_call(functools.partial(network_kernel, tiles=tiles), in_specs=[...  9.59 us
    pallas_call x1, Pallas kernels, forward(): pl.pallas_call(forward_kernel, in_specs=[pl.BlockSpec(memory_space=pltpu....  6.24 us
    pallas_call x1, Pallas kernels, adjoint(): pl.pallas_call(adjoint_kernel, in_specs=[pl.BlockSpec(memory_space=pltpu....  5.34 us
  transfers between devices with their start and end apart: 3, of which 3 were waited for; matrix products, arithmetic and copies ran while one was open for 0% of the time, Pallas kernels for 36%

profile of v4, /device:TPU:1, one launch (start us, length us, event | category | flops | bytes accessed | tf_op | source)
XLA Modules:
  0.0 118.5 jit_solution(17148785231128873617)
XLA Ops:
  0.6 6.2 %forward_dynamics.1 = bf16[4,32,4,16,128]{4,3,2,1,0:T(8,128)(2,1)} custom-call(bf16[2,1024,512]{2,1,0:T(8,128)(2,1)} %bitcast.16, bf16[1024,1024]{1,0:T(8,128)(2,1)} %op_hbm.3), custom_call_target="tpu_custom_call" | custom-call | flops 2147483648 | bytes 6291456 | tf_op jit(solution)/shard_map/forward_dynamics/pallas_call | solution.py:113
  6.9 11.5 %all-to-all-start = ((bf16[128,4,16,128]{3,2,1,0:T(8,128)(2,1)}), bf16[128,4,16,128]{3,2,1,0:T(8,128)(2,1)S(1)}, u32[]{:S(2)}, u32[]{:S(2)}) async-start(bf16[128,4,16,128]{3,2,1,0:T(8,128)(2,1)} %bitcast.14), calls=%async_computation | async-start | bytes 4194304 | tf_op jit(solution)/shard_map/all_to_all | solution.py:482
  18.4 0.0 copy-start.2
  18.4 0.0 copy-start.1
  18.4 13.4 %grad_mixed.1.gm_hbm = bf16[256,4096]{1,0:T(8,128)(2,1)} custom-call(bf16[32,32,4096]{2,1,0:T(8,128)(2,1)} %bitcast.10, bf16[256,4096]{1,0:T(8,128)(2,1)} %bitcast.15), custom_call_target="tpu_custom_call" | custom-call | flops 67108864 | bytes 16777216 | tf_op jit(solution)/shard_map/grad_mixed/pallas_call | solution.py:158
  31.8 0.0 copy-done.2
  31.8 0.0 copy-start
  31.9 17.0 %all-to-all-done.arrived = bf16[128,4,16,128]{3,2,1,0:T(8,128)(2,1)S(1)} async-done(((bf16[128,4,16,128]{3,2,1,0:T(8,128)(2,1)}), bf16[128,4,16,128]{3,2,1,0:T(8,128)(2,1)S(1)}, u32[]{:S(2)}, u32[]{:S(2)}) %all-to-all-start) | async-done | bytes 2097184 | tf_op jit(solution)/shard_map/all_to_all | solution.py:482
  48.9 0.0 copy-done.1
  48.9 9.6 %column_network.1 = (bf16[128,5,16,128]{3,2,1,0:T(8,128)(2,1)}, bf16[256,4096]{1,0:T(8,128)(2,1)}) custom-call(bf16[128,4,16,128]{3,2,1,0:T(8,128)(2,1)S(1)} %all-to-all-done.arrived, bf16[256,4096]{1,0:T(8,128)(2,1)} %grad_mixed.1.gm_hbm, bf16[512,256]{1,0:T(8,128)(2,1)S(1)} %broadcast_multiply_fusion.w_half.w_half_ref, bf16[256,512]{1,0:T(8,128)(2,1)S(1)} %copy-done.1), custom_call_target="tpu_custom_call" | custom-call | flops 4294967296 | bytes 14680064 | tf_op jit(solution)/shard_map/column_network/pallas_call | solution.py:261
  58.5 0.0 copy-done
  58.5 4.0 %all-to-all-start.1 = ((bf16[128,5,16,128]{3,2,1,0:T(8,128)(2,1)}), bf16[128,5,16,128]{3,2,1,0:T(8,128)(2,1)S(1)}, u32[]{:S(2)}, u32[]{:S(2)}) async-start(bf16[128,5,16,128]{3,2,1,0:T(8,128)(2,1)} %get-tuple-element.9), calls=%async_computation.1 | async-start | bytes 5242880 | tf_op jit(solution)/shard_map/all_to_all | solution.py:482
  62.5 23.7 %diffused.1._ = f32[8,32,4096]{2,1,0:T(8,128)} custom-call(bf16[256,4096]{1,0:T(8,128)(2,1)} %get-tuple-element.8.cols_ref, bf16[512,256]{1,0:T(8,128)(2,1)} %copy-done, bf16[256,512]{1,0:T(8,128)(2,1)} %w_out_ref.1, bf16[32,32,4096]{2,1,0:T(8,128)(2,1)} %bitcast.11), custom_call_target="tpu_custom_call" | custom-call | flops 2214592512 | bytes 16777216 | tf_op jit(solution)/shard_map/diffused/pallas_call | solution.py:320
  86.2 12.4 %all-to-all-done.1.returned = bf16[128,5,16,128]{3,2,1,0:T(8,128)(2,1)S(1)} async-done(((bf16[128,5,16,128]{3,2,1,0:T(8,128)(2,1)}), bf16[128,5,16,128]{3,2,1,0:T(8,128)(2,1)S(1)}, u32[]{:S(2)}, u32[]{:S(2)}) %all-to-all-start.1) | async-done | bytes 2621472 | tf_op jit(solution)/shard_map/all_to_all | solution.py:482
  98.6 0.9 weight_sum.1
  99.5 4.1 %all-to-all-start.2 = ((bf16[128,16,128]{2,1,0:T(8,128)(2,1)}), bf16[128,16,128]{2,1,0:T(8,128)(2,1)S(1)}, u32[]{:S(2)}, u32[]{:S(2)}) async-start(bf16[128,16,128]{2,1,0:T(8,128)(2,1)} %weight_sum.1), calls=%async_computation.2 | async-start | bytes 1048576 | tf_op jit(solution)/shard_map/all_to_all | solution.py:482
  103.6 5.3 %adjoint_dynamics.1 = f32[2,1024,512]{2,1,0:T(8,128)} custom-call(bf16[4,32,5,16,128]{4,3,2,1,0:T(8,128)(2,1)S(1)} %bitcast.9, bf16[1024,1024]{1,0:T(8,128)(2,1)} %op_hbm.3), custom_call_target="tpu_custom_call" | custom-call | flops 2147483648 | bytes 8388608 | tf_op jit(solution)/shard_map/adjoint_dynamics/pallas_call | solution.py:384
  109.0 8.5 %all-to-all-done.2.shares = bf16[128,16,128]{2,1,0:T(8,128)(2,1)S(1)} async-done(((bf16[128,16,128]{2,1,0:T(8,128)(2,1)}), bf16[128,16,128]{2,1,0:T(8,128)(2,1)S(1)}, u32[]{:S(2)}, u32[]{:S(2)}) %all-to-all-start.2) | async-done | bytes 524320 | tf_op jit(solution)/shard_map/all_to_all | solution.py:482
  117.4 1.0 weight_spread.1
  (1 shorter events, 0.0 us)
Async XLA Ops:
  6.9 42.0 %all-to-all-start = ((bf16[128,4,16,128]{3,2,1,0:T(8,128)(2,1)}), bf16[128,4,16,128]{3,2,1,0:T(8,128)(2,1)S(1)}, u32[]{:S(2)}, u32[]{:S(2)}) async-start(bf16[128,4,16,128]{3,2,1,0:T(8,128)(2,1)} %bitcast.14), calls=%async_computation | async-start | bytes 4194304 | tf_op jit(solution)/shard_map/all_to_all | solution.py:482
  18.4 13.4 %copy-start.2 = (bf16[512,256]{1,0:T(8,128)(2,1)S(1)}, bf16[512,256]{1,0:T(8,128)(2,1)}, u32[]{:S(2)}) copy-start(bf16[512,256]{1,0:T(8,128)(2,1)} %param.8) | copy-start | bytes 786436
  18.4 30.5 %copy-start.1 = (bf16[256,512]{1,0:T(8,128)(2,1)S(1)}, bf16[256,512]{1,0:T(8,128)(2,1)}, u32[]{:S(2)}) copy-start(bf16[256,512]{1,0:T(8,128)(2,1)} %w_out_ref.1) | copy-start | bytes 786436
  31.8 26.6 %copy-start = (bf16[512,256]{1,0:T(8,128)(2,1)}, bf16[512,256]{1,0:T(8,128)(2,1)S(1)}, u32[]{:S(2)}) copy-start(bf16[512,256]{1,0:T(8,128)(2,1)S(1)} %broadcast_multiply_fusion.w_half.w_half_ref) | copy-start | bytes 786436
  58.5 40.1 %all-to-all-start.1 = ((bf16[128,5,16,128]{3,2,1,0:T(8,128)(2,1)}), bf16[128,5,16,128]{3,2,1,0:T(8,128)(2,1)S(1)}, u32[]{:S(2)}, u32[]{:S(2)}) async-start(bf16[128,5,16,128]{3,2,1,0:T(8,128)(2,1)} %get-tuple-element.9), calls=%async_computation.1 | async-start | bytes 5242880 | tf_op jit(solution)/shard_map/all_to_all | solution.py:482
  99.5 17.9 %all-to-all-start.2 = ((bf16[128,16,128]{2,1,0:T(8,128)(2,1)}), bf16[128,16,128]{2,1,0:T(8,128)(2,1)S(1)}, u32[]{:S(2)}, u32[]{:S(2)}) async-start(bf16[128,16,128]{2,1,0:T(8,128)(2,1)} %weight_sum.1), calls=%async_computation.2 | async-start | bytes 1048576 | tf_op jit(solution)/shard_map/all_to_all | solution.py:482

commit v5 on v4

--- a/solution.py
+++ b/solution.py
@@ -65,9 +65,14 @@
     def fetch_v(f):
         return pltpu.make_async_copy(v_hbm.at[f], v_ref.at[f], v_sem.at[f])
 
-    def store(i):
-        part = pl.ds(i * per_block, per_block)
-        return pltpu.make_async_copy(out_ref.at[:, part], out_hbm.at[:, part], out_sem.at[i])
+    half = tiles // 2
+    width = half * LANES
+
+    def store(k):
+        across, part = pl.ds((k % 2) * half, half), pl.ds((k // 2) * per_block, per_block)
+        return pltpu.make_async_copy(
+            out_ref.at[across, part], out_hbm.at[across, part], out_sem.at[k]
+        )
 
     for f in range(fields):
         fetch_v(f).start()
@@ -81,27 +86,32 @@
         return carry
 
     lax.fori_loop(0, fields, across, 0)
-    def step(i, carry):
-        fetch_op(i).wait()
+    def step(k, carry):
+        i, h = k // 2, k % 2
+
+        @pl.when(h == 0)
+        def _():
+            fetch_op(i).wait()
 
         rows_here = pl.ds(pl.multiple_of(i * block, block), block)
+        lanes = pl.ds(pl.multiple_of(h * width, width), width)
         done = []
         for f in range(fields):
-            along = dot(op_ref[i], v_ref[f], (0, 0))
-            done.append(along + side[f, rows_here, :])
-        for a in range(tiles):
+            along = dot(op_ref[i], v_ref[f, :, lanes], (0, 0))
+            done.append(along + side[f, rows_here, lanes])
+        for a in range(half):
             parts = [
                 d[:, a * LANES : (a + 1) * LANES].reshape(per_block, chunks, 1, QROWS, LANES)
                 for d in done
             ]
             joined = jnp.concatenate(parts, axis=2).reshape(per_block, chunks, rows, LANES)
-            out_ref[a, pl.ds(i * per_block, per_block)] = joined.astype(BF)
-        store(i).start()
+            out_ref[h * half + a, pl.ds(i * per_block, per_block)] = joined.astype(BF)
+        store(k).start()
         return carry
 
-    lax.fori_loop(0, blocks, step, 0)
-    for i in range(blocks):
-        store(i).wait()
+    lax.fori_loop(0, 2 * blocks, step, 0)
+    for k in range(2 * blocks):
+        store(k).wait()
 
 
 def forward(fields_in, operator, lat_tiles, lon_tiles, tile_lon):
@@ -123,7 +133,7 @@
             pltpu.VMEM(fields_in.shape, F32),
             pltpu.SemaphoreType.DMA((fields,)),
             pltpu.SemaphoreType.DMA((blocks,)),
-            pltpu.SemaphoreType.DMA((blocks,)),
+            pltpu.SemaphoreType.DMA((2 * blocks,)),
         ],
         compiler_params=params(),
         cost_estimate=cost(2 * fields * grid_lon * grid_lon * grid_lat, 6 << 20),

time: 119 us -> 119 us (level)
  no operation moved by 1% of the time
where the time goes in v5:
time: 119 us
  Pallas kernels  60.5 us (51%)
  waiting for transfers between devices  37.9 us (32%)
  starting transfers between devices  19.6 us (16%)
    all_to_all x3, waiting for transfers between devices, exchange(): return lax.all_to_all(array, AXES, split_axis=0, concat_axis=0, tiled=True)  37.9 us
    pallas_call x1, Pallas kernels, diffused_of(): pl.pallas_call(diffused_kernel, grid=(columns // chunk,), in_specs=[pl.Bl...  23.7 us
    all_to_all x3, starting transfers between devices, exchange(): return lax.all_to_all(array, AXES, split_axis=0, concat_axis=0, tiled=True)  19.6 us
    pallas_call x1, Pallas kernels, grad_mixed_of(): pl.pallas_call(grad_mixed_kernel, grid=(columns // chunk,), in_specs=[pl....  13.4 us
    pallas_call x1, Pallas kernels, network(): pl.pallas_call(functools.partial(network_kernel, tiles=tiles), in_specs=[...  9.59 us
    pallas_call x1, Pallas kernels, forward(): pl.pallas_call(forward_kernel, in_specs=[pl.BlockSpec(memory_space=pltpu....  6.49 us
    pallas_call x1, Pallas kernels, adjoint(): pl.pallas_call(adjoint_kernel, in_specs=[pl.BlockSpec(memory_space=pltpu....  5.34 us
  transfers between devices with their start and end apart: 3, of which 3 were waited for; matrix products, arithmetic and copies ran while one was open for 0% of the time, Pallas kernels for 36%

profile of v5, /device:TPU:1, one launch (start us, length us, event | category | flops | bytes accessed | tf_op | source)
XLA Modules:
  0.0 118.7 jit_solution(6918535542842516118)
XLA Ops:
  0.6 6.5 %forward_dynamics.1 = bf16[4,32,4,16,128]{4,3,2,1,0:T(8,128)(2,1)} custom-call(bf16[2,1024,512]{2,1,0:T(8,128)(2,1)} %bitcast.16, bf16[1024,1024]{1,0:T(8,128)(2,1)} %op_hbm.3), custom_call_target="tpu_custom_call" | custom-call | flops 2147483648 | bytes 6291456 | tf_op jit(solution)/shard_map/forward_dynamics/pallas_call | solution.py:123
  7.1 11.5 %all-to-all-start = ((bf16[128,4,16,128]{3,2,1,0:T(8,128)(2,1)}), bf16[128,4,16,128]{3,2,1,0:T(8,128)(2,1)S(1)}, u32[]{:S(2)}, u32[]{:S(2)}) async-start(bf16[128,4,16,128]{3,2,1,0:T(8,128)(2,1)} %bitcast.14), calls=%async_computation | async-start | bytes 4194304 | tf_op jit(solution)/shard_map/all_to_all | solution.py:492
  18.6 0.0 copy-start.2
  18.6 0.0 copy-start.1
  18.6 13.4 %grad_mixed.1.gm_hbm = bf16[256,4096]{1,0:T(8,128)(2,1)} custom-call(bf16[32,32,4096]{2,1,0:T(8,128)(2,1)} %bitcast.10, bf16[256,4096]{1,0:T(8,128)(2,1)} %bitcast.15), custom_call_target="tpu_custom_call" | custom-call | flops 67108864 | bytes 16777216 | tf_op jit(solution)/shard_map/grad_mixed/pallas_call | solution.py:168
  32.1 0.0 copy-done.2
  32.1 0.0 copy-start
  32.1 17.0 %all-to-all-done.arrived = bf16[128,4,16,128]{3,2,1,0:T(8,128)(2,1)S(1)} async-done(((bf16[128,4,16,128]{3,2,1,0:T(8,128)(2,1)}), bf16[128,4,16,128]{3,2,1,0:T(8,128)(2,1)S(1)}, u32[]{:S(2)}, u32[]{:S(2)}) %all-to-all-start) | async-done | bytes 2097184 | tf_op jit(solution)/shard_map/all_to_all | solution.py:492
  49.1 0.0 copy-done.1
  49.1 9.6 %column_network.1 = (bf16[128,5,16,128]{3,2,1,0:T(8,128)(2,1)}, bf16[256,4096]{1,0:T(8,128)(2,1)}) custom-call(bf16[128,4,16,128]{3,2,1,0:T(8,128)(2,1)S(1)} %all-to-all-done.arrived, bf16[256,4096]{1,0:T(8,128)(2,1)} %grad_mixed.1.gm_hbm, bf16[512,256]{1,0:T(8,128)(2,1)S(1)} %broadcast_multiply_fusion.w_half.w_half_ref, bf16[256,512]{1,0:T(8,128)(2,1)S(1)} %copy-done.1), custom_call_target="tpu_custom_call" | custom-call | flops 4294967296 | bytes 14680064 | tf_op jit(solution)/shard_map/column_network/pallas_call | solution.py:271
  58.7 0.0 copy-done
  58.7 4.0 %all-to-all-start.1 = ((bf16[128,5,16,128]{3,2,1,0:T(8,128)(2,1)}), bf16[128,5,16,128]{3,2,1,0:T(8,128)(2,1)S(1)}, u32[]{:S(2)}, u32[]{:S(2)}) async-start(bf16[128,5,16,128]{3,2,1,0:T(8,128)(2,1)} %get-tuple-element.9), calls=%async_computation.1 | async-start | bytes 5242880 | tf_op jit(solution)/shard_map/all_to_all | solution.py:492
  62.7 23.7 %diffused.1._ = f32[8,32,4096]{2,1,0:T(8,128)} custom-call(bf16[256,4096]{1,0:T(8,128)(2,1)} %get-tuple-element.8.cols_ref, bf16[512,256]{1,0:T(8,128)(2,1)} %copy-done, bf16[256,512]{1,0:T(8,128)(2,1)} %w_out_ref.1, bf16[32,32,4096]{2,1,0:T(8,128)(2,1)} %bitcast.11), custom_call_target="tpu_custom_call" | custom-call | flops 2214592512 | bytes 16777216 | tf_op jit(solution)/shard_map/diffused/pallas_call | solution.py:330
  86.4 12.4 %all-to-all-done.1.returned = bf16[128,5,16,128]{3,2,1,0:T(8,128)(2,1)S(1)} async-done(((bf16[128,5,16,128]{3,2,1,0:T(8,128)(2,1)}), bf16[128,5,16,128]{3,2,1,0:T(8,128)(2,1)S(1)}, u32[]{:S(2)}, u32[]{:S(2)}) %all-to-all-start.1) | async-done | bytes 2621472 | tf_op jit(solution)/shard_map/all_to_all | solution.py:492
  98.8 0.9 weight_sum.1
  99.7 4.1 %all-to-all-start.2 = ((bf16[128,16,128]{2,1,0:T(8,128)(2,1)}), bf16[128,16,128]{2,1,0:T(8,128)(2,1)S(1)}, u32[]{:S(2)}, u32[]{:S(2)}) async-start(bf16[128,16,128]{2,1,0:T(8,128)(2,1)} %weight_sum.1), calls=%async_computation.2 | async-start | bytes 1048576 | tf_op jit(solution)/shard_map/all_to_all | solution.py:492
  103.8 5.3 %adjoint_dynamics.1 = f32[2,1024,512]{2,1,0:T(8,128)} custom-call(bf16[4,32,5,16,128]{4,3,2,1,0:T(8,128)(2,1)S(1)} %bitcast.9, bf16[1024,1024]{1,0:T(8,128)(2,1)} %op_hbm.3), custom_call_target="tpu_custom_call" | custom-call | flops 2147483648 | bytes 8388608 | tf_op jit(solution)/shard_map/adjoint_dynamics/pallas_call | solution.py:394
  109.2 8.5 %all-to-all-done.2.shares = bf16[128,16,128]{2,1,0:T(8,128)(2,1)S(1)} async-done(((bf16[128,16,128]{2,1,0:T(8,128)(2,1)}), bf16[128,16,128]{2,1,0:T(8,128)(2,1)S(1)}, u32[]{:S(2)}, u32[]{:S(2)}) %all-to-all-start.2) | async-done | bytes 524320 | tf_op jit(solution)/shard_map/all_to_all | solution.py:492
  117.7 1.0 weight_spread.1
  (1 shorter events, 0.0 us)
Async XLA Ops:
  7.1 42.0 %all-to-all-start = ((bf16[128,4,16,128]{3,2,1,0:T(8,128)(2,1)}), bf16[128,4,16,128]{3,2,1,0:T(8,128)(2,1)S(1)}, u32[]{:S(2)}, u32[]{:S(2)}) async-start(bf16[128,4,16,128]{3,2,1,0:T(8,128)(2,1)} %bitcast.14), calls=%async_computation | async-start | bytes 4194304 | tf_op jit(solution)/shard_map/all_to_all | solution.py:492
  18.6 13.4 %copy-start.2 = (bf16[512,256]{1,0:T(8,128)(2,1)S(1)}, bf16[512,256]{1,0:T(8,128)(2,1)}, u32[]{:S(2)}) copy-start(bf16[512,256]{1,0:T(8,128)(2,1)} %param.8) | copy-start | bytes 786436
  18.6 30.5 %copy-start.1 = (bf16[256,512]{1,0:T(8,128)(2,1)S(1)}, bf16[256,512]{1,0:T(8,128)(2,1)}, u32[]{:S(2)}) copy-start(bf16[256,512]{1,0:T(8,128)(2,1)} %w_out_ref.1) | copy-start | bytes 786436
  32.1 26.6 %copy-start = (bf16[512,256]{1,0:T(8,128)(2,1)}, bf16[512,256]{1,0:T(8,128)(2,1)S(1)}, u32[]{:S(2)}) copy-start(bf16[512,256]{1,0:T(8,128)(2,1)S(1)} %broadcast_multiply_fusion.w_half.w_half_ref) | copy-start | bytes 786436
  58.7 40.1 %all-to-all-start.1 = ((bf16[128,5,16,128]{3,2,1,0:T(8,128)(2,1)}), bf16[128,5,16,128]{3,2,1,0:T(8,128)(2,1)S(1)}, u32[]{:S(2)}, u32[]{:S(2)}) async-start(bf16[128,5,16,128]{3,2,1,0:T(8,128)(2,1)} %get-tuple-element.9), calls=%async_computation.1 | async-start | bytes 5242880 | tf_op jit(solution)/shard_map/all_to_all | solution.py:492
  99.7 17.9 %all-to-all-start.2 = ((bf16[128,16,128]{2,1,0:T(8,128)(2,1)}), bf16[128,16,128]{2,1,0:T(8,128)(2,1)S(1)}, u32[]{:S(2)}, u32[]{:S(2)}) async-start(bf16[128,16,128]{2,1,0:T(8,128)(2,1)} %weight_sum.1), calls=%async_computation.2 | async-start | bytes 1048576 | tf_op jit(solution)/shard_map/all_to_all | solution.py:492
